TPU v7x, 32 devices: a whole 2x2x4 slice. The times are simulated.
32 devices in a mesh: dp: 2 (over y), panel: 16 (over z, x, core).
Axes of the slice: x: 2, y: 2, z: 4, core: 2. Of those that a mesh axis runs over, the one named last changes fastest.
Arguments:
- tokens: bfloat16 [512, 6144], P('dp'), may hold values from -8 to 8
- out_grads: bfloat16 [512, 6144], P('dp'), may hold values from -8 to 8
- basis_in: bfloat16 [6144, 6144], P(None, 'panel'), may hold values from -0.078125 to 0.078125
- basis_out: bfloat16 [6144, 6144], P(None, 'panel'), may hold values from -0.078125 to 0.078125
Outputs:
- update: bfloat16 [6144, 6144], P('panel', 'dp')
All inputs are finite; a program needn't handle non-finite values.
Results may differ from a plain program's by a relative error of at most 0.012.
Values may be sent and summed in bfloat16 or wider, within the bound.
No kernel may reach another device: no remote copies, remote signals or barrier semaphores. Data moves between devices by JAX's collectives and lax.ppermute only.
A program may use at most 128 MiB of HBM per device.

v0:
```python
import jax
import jax.numpy as jnp
from jax import lax
from jax.sharding import PartitionSpec as P

damping = 0.1


def shards(tokens, out_grads, basis_in, basis_out):
    rows_dev = tokens.shape[0]
    tok_total = rows_dev * lax.axis_size("dp")
    row_block = basis_in.shape[0] // lax.axis_size("dp")
    proj_in = jnp.dot(tokens, basis_in, preferred_element_type=jnp.float32).astype(jnp.bfloat16)
    proj_out = jnp.dot(out_grads, basis_out, preferred_element_type=jnp.float32).astype(
        jnp.bfloat16
    )
    sq_in = (proj_in.astype(jnp.float32) ** 2).astype(jnp.bfloat16)
    sq_out = (proj_out.astype(jnp.float32) ** 2).astype(jnp.bfloat16)
    stacked = jnp.concatenate([proj_out, sq_out], axis=0)
    contract = (((0,), (0,)), ((), ()))
    segment = lax.all_gather(stacked, "panel", axis=1, tiled=True)
    product = lax.dot_general(
        proj_in, segment[:rows_dev], contract, preferred_element_type=jnp.float32
    )
    square = lax.dot_general(
        sq_in, segment[rows_dev:], contract, preferred_element_type=jnp.float32
    )
    partials = jnp.stack([product, square]) / tok_total
    shares = lax.psum_scatter(
        partials.astype(jnp.bfloat16), "dp", scatter_dimension=2, tiled=True
    ).astype(jnp.float32)
    local_ratio = (shares[0] / (shares[1] + damping)).astype(jnp.bfloat16)
    ratio = lax.all_gather(local_ratio, "dp", axis=1, tiled=True)
    first_row = lax.axis_index("dp") * row_block
    out_rows = lax.dynamic_slice_in_dim(basis_out, first_row, row_block, 0)
    columns = ratio
    rotated = lax.dot_general(
        columns,
        lax.all_gather(out_rows, "panel", axis=1, tiled=True),
        (((1,), (1,)), ((), ())),
        preferred_element_type=jnp.float32,
    ).astype(jnp.bfloat16)
    in_rows = lax.all_to_all(basis_in, "panel", split_axis=0, concat_axis=1, tiled=True)
    columns = in_rows
    update = jnp.dot(
        columns,
        lax.all_gather(rotated, "panel", axis=0, tiled=True),
        preferred_element_type=jnp.float32,
    )
    return update.astype(jnp.bfloat16)


def solution(mesh):
    return jax.shard_map(
        shards,
        mesh=mesh,
        in_specs=(P("dp", None), P("dp", None), P(None, "panel"), P(None, "panel")),
        out_specs=P("panel", "dp"),
        check_vma=False,
    )
```

profile of v0, /device:TPU:9, one launch (start us, length us, event | category | flops | bytes accessed | tf_op | source)
XLA Modules:
  0.0 804.2 jit_solution(10812107732864825108)
XLA Ops:
  6.5 0.0 copy-start
  6.5 1.9 copy-done
  8.4 4.1 multiply_convert_fusion.1
  12.6 0.8 pad_maximum_fusion
  13.4 0.0 all-gather.6.cloned.1.call-update
  13.4 0.0 reduce-scatter.2.cloned.1.call-start
  13.4 5.1 convolution_convert_fusion.2
  18.5 60.4 %all-gather.6.cloned.1.call-done = bf16[512,6144]{1,0:T(8,128)(2,1)} async-done(((bf16[512,384]{1,0:T(8,128)(2,1)}), bf16[512,6144]{1,0:T(8,128)(2,1)}) %all-gather.6.cloned.1.call-update) | async-done | bytes 6291472 | tf_op jit(solution)/shard_map/all_gather | solution.py:21
  78.9 3.5 convolution_bitcast_fusion
  82.4 0.3 copy-done.2
  82.7 1.4 convolution_bitcast_fusion.1
  84.1 4.3 fusion
  88.4 0.0 reduce-scatter.2.cloned.1.call-update
  88.4 0.0 all-gather.12.cloned.1.call-start
  88.5 110.3 %reduce-scatter.2.cloned.1.call-done = bf16[2,384,3072]{2,1,0:T(8,128)(2,1)} async-done(((bf16[2,384,6144]{2,1,0:T(8,128)(2,1)}), bf16[2,384,3072]{2,1,0:T(8,128)(2,1)}) %reduce-scatter.2.cloned.1.call-update) | async-done | bytes 4718608 | tf_op jit(solution)/shard_map/reduce_scatter | solution.py:29
  198.7 3.6 convert_element_type.46
  202.3 2.3 fusion.2
  204.6 0.0 all-gather.12.cloned.1.call-update
  204.7 0.0 all-gather.8.cloned.1.call-start
  204.7 3.3 constant_dynamic-slice_fusion
  208.0 0.0 all-gather.8.cloned.1.call-update
  208.1 0.2 all-gather.10.cloned.1.call-start
  208.3 59.2 %all-gather.12.cloned.1.call-done = bf16[1,384,6144]{2,1,0:T(8,128)(2,1)} async-done(((bf16[1,384,3072]{2,1,0:T(8,128)(2,1)}), bf16[1,384,6144]{2,1,0:T(8,128)(2,1)}) %all-gather.12.cloned.1.call-update) | async-done | bytes 4718608 | tf_op jit(solution)/shard_map/all_gather | solution.py:33
  267.5 189.4 %all-gather.8.cloned.1.call-done = bf16[3072,6144]{1,0:T(8,128)(2,1)} async-done(((bf16[3072,384]{1,0:T(8,128)(2,1)}), bf16[3072,6144]{1,0:T(8,128)(2,1)}) %all-gather.8.cloned.1.call-update) | async-done | bytes 37748752 | tf_op jit(solution)/shard_map/all_gather | solution.py:39
  456.9 22.0 %fusion.5 = bf16[384,3072]{1,0:T(8,128)(2,1)} fusion(bf16[3072,6144]{1,0:T(8,128)(2,1)} %all-gather.8.cloned.1.call-done, bf16[1,384,6144]{2,1,0:T(8,128)(2,1)} %all-gather.12.cloned.1.call-done), kind=kOutput, calls=%fused_computation.9 | convolution fusion | flops 14496694272 | bytes 44826624 | tf_op jit(solution)/shard_map/dot_general | solution.py:37
  478.9 0.0 all-gather.10.cloned.1.call-update
  478.9 158.3 %all_to_all.19 = bf16[16,384,384]{2,1,0:T(8,128)(2,1)} all-to-all(bf16[16,384,384]{2,1,0:T(8,128)(2,1)} %bitcast.23), channel_id=1, replica_groups=mesh['dp'=2,'panel'=16] {'panel'}, dimensions={0} | all-to-all | bytes 9437184 | tf_op jit(solution)/shard_map/all_to_all | solution.py:43
  637.2 6.7 copy.7
  643.9 123.3 %all-gather.10.cloned.1.call-done = bf16[6144,3072]{1,0:T(8,128)(2,1)} async-done(((bf16[384,3072]{1,0:T(8,128)(2,1)}), bf16[6144,3072]{1,0:T(8,128)(2,1)}) %all-gather.10.cloned.1.call-update) | async-done | bytes 37748752 | tf_op jit(solution)/shard_map/all_gather | solution.py:47
  767.2 26.2 %fusion.8 = bf16[384,3072]{0,1:T(8,128)(2,1)} fusion(bf16[6144,3072]{1,0:T(8,128)(2,1)} %all-gather.10.cloned.1.call-done, bf16[384,6144]{0,1:T(8,128)(2,1)} %bitcast.24), kind=kOutput, calls=%fused_computation.11 | convolution fusion | flops 14496694272 | bytes 44826624 | tf_op jit(solution)/shard_map/dot_general | solution.py:45
  793.4 4.3 copy.8
  797.7 0.0 copy-done.1
  (3 shorter events, 0.0 us)
Async XLA Ops:
  6.5 1.9 copy-start
  6.5 72.4 %all-gather.6.cloned.1.call-start = ((), (), s32[]{:S(2)}) async-start(), calls=%async_computation.2 | async-start | bytes 6684672 | tf_op jit(solution)/shard_map/all_gather | solution.py:21
  13.4 185.4 %reduce-scatter.2.cloned.1.call-start = ((), (), s32[]{:S(2)}) async-start(), calls=%async_computation.3 | async-start | bytes 14155776 | tf_op jit(solution)/shard_map/reduce_scatter | solution.py:29
  78.9 3.7 copy-start.2
  88.4 179.1 %all-gather.12.cloned.1.call-start = ((), (), s32[]{:S(2)}) async-start(), calls=%async_computation.6 | async-start | bytes 7077888 | tf_op jit(solution)/shard_map/all_gather | solution.py:33
  204.7 252.2 %all-gather.8.cloned.1.call-start = ((), (), s32[]{:S(2)}) async-start(), calls=%async_computation.4 | async-start | bytes 40108032 | tf_op jit(solution)/shard_map/all_gather | solution.py:39
  208.1 559.1 %all-gather.10.cloned.1.call-start = ((), (), s32[]{:S(2)}) async-start(), calls=%async_computation.5 | async-start | bytes 40108032 | tf_op jit(solution)/shard_map/all_gather | solution.py:47
  767.2 30.5 %copy-start.1 = (bf16[256,6144]{1,0:T(8,128)(2,1)S(1)}, bf16[256,6144]{1,0:T(8,128)(2,1)}, u32[]{:S(2)}) copy-start(bf16[256,6144]{1,0:T(8,128)(2,1)} %param.5) | copy-start | bytes 9437188
Sparse Core Ops, SparseCore 0:
  13.5 65.3 all-gather.5
  88.5 110.1 reduce-scatter.1
  204.8 62.6 all-gather.11
  268.9 187.9 all-gather.7
  479.0 288.0 all-gather.9
where the time goes:
time: 805 us; the launch traced here: 804 us
  waiting for transfers between devices  543 us (67%)
  blocking collectives  158 us (20%)
  matrix products  62.3 us (8%)
  local copies, waits for them, and re-layouts  16.4 us (2%)
  between operations  13.2 us (2%)
  other arithmetic  11 us (1%)
    all_gather x1, waiting for transfers between devices, shards(): lax.all_gather(out_rows, 'panel', axis=1, tiled=True)  189 us
    all_to_all x1, blocking collectives, shards(): lax.all_to_all(basis_in, 'panel', split_axis=0, concat_axis=1, tiled=True)  158 us
    all_gather x1, waiting for transfers between devices, shards(): lax.all_gather(rotated, 'panel', axis=0, tiled=True)  123 us
    reduce_scatter x1, waiting for transfers between devices, shards(): lax.psum_scatter(partials.astype(jnp.bfloat16), 'dp', scatter_dimension=2...  110 us
    all_gather x1, waiting for transfers between devices, shards(): segment = lax.all_gather(stacked, 'panel', axis=1, tiled=True)  60.4 us
    all_gather x1, waiting for transfers between devices, shards(): ratio = lax.all_gather(local_ratio, 'dp', axis=1, tiled=True)  59.2 us
    dot_general x1, matrix products, shards(): jnp.dot(columns, lax.all_gather(rotated, 'panel', axis=0, tiled=True), pr...  26.2 us
    dot_general x1, matrix products, shards(): lax.dot_general(columns, lax.all_gather(out_rows, 'panel', axis=1, tiled=...  22 us
  transfers between devices with their start and end apart: 5, of which 5 were waited for; matrix products, arithmetic and copies ran while one was open for 2% of the time, Pallas kernels for 0%

commit v1 on v0

v1 whole, which is shorter than its diff:
```python
import jax
import jax.numpy as jnp
from jax import lax
from jax.sharding import PartitionSpec as P

damping = 0.1
pair = 2
chunks = 4
f32 = jnp.float32
bf16 = jnp.bfloat16


class Grid:
    def __init__(self):
        self.panel = lax.axis_size("panel")
        self.dp = lax.axis_size("dp")
        self.sizes = {"z": self.panel // (pair * pair), "x": pair, "c": pair}
        self.steps = {"z": pair * pair, "x": pair, "c": 1}
        p = lax.axis_index("panel")
        self.at = {k: (p // self.steps[k]) % self.sizes[k] for k in self.sizes}
        self.at["y"] = lax.axis_index("dp")
        self.sizes["y"] = self.dp

    def pairs(self, axis, shift, keep=None):
        size = self.sizes[axis]
        if axis == "y":
            return [((i + shift) % size, i) for i in range(size)]
        step = self.steps[axis]
        out = []
        for q in range(self.panel):
            i = (q // step) % size
            j = (i + shift) % size
            if keep is None or keep(j, i):
                out.append((q + (j - i) * step, q))
        return out

    def fetch(self, value, axis, shift, keep=None):
        name = "dp" if axis == "y" else "panel"
        return lax.ppermute(value, name, self.pairs(axis, shift, keep))

    def gather(self, value, axis):
        return [value] + [self.fetch(value, axis, s) for s in range(1, self.sizes[axis])]

    def gather_line(self, value):
        n = self.sizes["z"]
        if n < 4:
            return self.gather(value, "z")
        z = self.at["z"]
        out = {0: value}
        for s in list(range(2, n - 1)) + [1, n - 1]:
            out[s] = self.fetch(value, "z", s, lambda j, i: abs(j - i) < n - 1)
        relay = out[2] if n == 4 else jnp.where(z == 1, out[n - 2], out[2])
        ends = lambda j, i: (j, i) == (1, 0)
        low = set(self.pairs("z", 1, ends))
        high = set(self.pairs("z", n - 1, lambda j, i: (j, i) == (n - 2, n - 1)))
        far = lax.ppermute(relay, "panel", sorted(low | high))
        out[1] = jnp.where(z == n - 1, far, out[1])
        out[n - 1] = jnp.where(z == 0, far, out[n - 1])
        return [out[s] for s in range(n)]


def dot(a, b, contract):
    return lax.dot_general(a, b, (contract, ((), ())), preferred_element_type=f32)


def shards(tokens, out_grads, basis_in, basis_out):
    grid = Grid()
    at, sizes = grid.at, grid.sizes
    nz, ny = sizes["z"], sizes["y"]
    width, cols = basis_in.shape
    tok_total = tokens.shape[0] * ny

    quarter = width // nz
    eighth = quarter // ny
    in_blocks = []
    for s in range(nz):
        to = (at["z"] + nz - s) % nz
        block = lax.dynamic_slice_in_dim(basis_in, to * quarter + at["y"] * eighth, eighth, 0)
        in_blocks.append(block if s == 0 else grid.fetch(block, "z", s))
    in_rows = jnp.concatenate(in_blocks, axis=1)
    in_rows = jnp.concatenate(grid.gather(in_rows, "x"), axis=1)

    proj_in = jnp.dot(tokens, basis_in, preferred_element_type=f32).astype(bf16)
    proj_out = jnp.dot(out_grads, basis_out, preferred_element_type=f32).astype(bf16)
    both = jnp.concatenate([proj_in, proj_out], axis=0)
    both = jnp.concatenate(grid.gather_line(both), axis=1)
    both = jnp.stack(grid.gather(both, "y"))
    rows = tokens.shape[0]
    left = both[:, :rows].reshape(tok_total, -1)
    right = both[:, rows:].reshape(tok_total, -1)
    left = jnp.concatenate(grid.gather(left, "x"), axis=1)
    right = jnp.concatenate(grid.gather(right, "c"), axis=1)

    square = lambda v: (v.astype(f32) ** 2).astype(bf16)
    summed = dot(left, right, ((0,), (0,))) / tok_total
    corrections = dot(square(left), square(right), ((0,), (0,))) / tok_total
    ratio = (summed / (corrections + damping)).astype(bf16)

    part = dot(in_rows, ratio, ((1,), (0,)))
    half = part.shape[1] // sizes["c"]
    mixed = part[:, :half]
    for s in range(1, sizes["c"]):
        mixed = mixed + grid.fetch(part[:, s * half : (s + 1) * half].astype(bf16), "c", s).astype(f32)
    mixed = mixed.astype(bf16)
    full = jnp.zeros((quarter, half), bf16)
    for s, block in enumerate(grid.gather(mixed, "y")):
        full = lax.dynamic_update_slice_in_dim(full, block, ((at["y"] + s) % ny) * eighth, 0)

    own = quarter // (pair * pair)
    ordered = [
        lax.dynamic_slice_in_dim(
            full, (((at["x"] + i) % pair) * pair + (at["c"] + j) % pair) * own, own, 0
        )
        for j in range(pair)
        for i in range(pair)
    ]
    near = jnp.concatenate(ordered[:pair], axis=0)
    away = jnp.concatenate(ordered[pair:], axis=0)

    out_rows = width // ny
    step = out_rows // chunks
    done = []
    for k in range(chunks):
        block = lax.dynamic_slice_in_dim(basis_out, at["y"] * out_rows + k * step, step, 0)
        block = jnp.concatenate(grid.gather_line(block), axis=1)
        given = dot(away, block, ((1,), (1,))).astype(bf16)
        kept = dot(near, block, ((1,), (1,)))
        kept = kept + grid.fetch(given, "c", 1).astype(f32)
        other = grid.fetch(kept[own:].astype(bf16), "x", 1)
        done.append((kept[:own] + other.astype(f32)).astype(bf16))
    return jnp.concatenate(done, axis=1)


def solution(mesh):
    return jax.shard_map(
        shards,
        mesh=mesh,
        in_specs=(P("dp", None), P("dp", None), P(None, "panel"), P(None, "panel")),
        out_specs=P("panel", "dp"),
        check_vma=False,
    )
```

time: 805 us -> 532 us (0.66)
  waiting for transfers between devices: 543 us -> 322 us
  blocking collectives: 158 us -> 0 us
  starting transfers between devices: 0.35 us -> 72.8 us
  matrix products: 62.3 us -> 89.4 us
  between operations: 13.2 us -> 0.52 us
  local copies, waits for them, and re-layouts: 16.4 us -> 26.9 us
    all_gather x4 -> x0, waiting for transfers between devices: 432 us -> none  [the longest x1 189 us: shards(): lax.all_gather(out_rows, 'panel', axis=1, tiled=True)]
    ppermute x0 -> x37, waiting for transfers between devices: none -> 322 us  [the longest x32 283 us: fetch(): return lax.ppermute(value, name, self.pairs(axis, shift, keep))]
    all_to_all x1 -> x0, blocking collectives: 158 us -> none  [shards(): lax.all_to_all(basis_in, 'panel', split_axis=0, concat_axis=1, tiled=True)]
    reduce_scatter x1 -> x0, waiting for transfers between devices: 110 us -> none  [shards(): lax.psum_scatter(partials.astype(jnp.bfloat16), 'dp', scatter_dimension=2...]
    ppermute x0 -> x37, starting transfers between devices: none -> 72.8 us  [the longest x32 54.2 us: fetch(): return lax.ppermute(value, name, self.pairs(axis, shift, keep))]
    dot_general x6 -> x12, matrix products: 62.3 us -> 89.4 us  [the longest x10 83.4 us: dot(): lax.dot_general(a, b, (contract, ((), ())), preferred_element_type=f32)]
    convert_element_type x3 -> x4, other arithmetic: 10.2 us -> 0.53 us  [shards(): done.append((kept[:own] + other.astype(f32)).astype(bf16))]
  transfers between devices with their start and end apart: 5 -> 37, of which waited for: 5 -> 21; matrix products, arithmetic and copies ran while one was open for 2% -> 9% of each run, Pallas kernels for 0% -> 0%
where the time goes in v1:
time: 532 us; the launch traced here: 527 us
  waiting for transfers between devices  322 us (61%)
  matrix products  89.4 us (17%)
  starting transfers between devices  72.8 us (14%)
  local copies, waits for them, and re-layouts  26.9 us (5%)
  other arithmetic  15.2 us (3%)
    ppermute x32, waiting for transfers between devices, fetch(): return lax.ppermute(value, name, self.pairs(axis, shift, keep))  283 us
    dot_general x10, matrix products, dot(): lax.dot_general(a, b, (contract, ((), ())), preferred_element_type=f32)  83.4 us
    ppermute x32, starting transfers between devices, fetch(): return lax.ppermute(value, name, self.pairs(axis, shift, keep))  54.2 us
    ppermute x5, waiting for transfers between devices, gather_line(): far = lax.ppermute(relay, 'panel', sorted(low | high))  39.2 us
    ppermute x5, starting transfers between devices, gather_line(): far = lax.ppermute(relay, 'panel', sorted(low | high))  18.6 us
  transfers between devices with their start and end apart: 37, of which 21 were waited for; matrix products, arithmetic and copies ran while one was open for 9% of the time, Pallas kernels for 0%

profile of v1, /device:TPU:9, one launch (start us, length us, event | category | flops | bytes accessed | tf_op | source)
XLA Modules:
  0.0 527.3 jit_solution(15494450737406220330)
XLA Ops:
  1.9 4.3 convolution_convert_fusion.4
  16.4 12.2 %collective-permute-done.4 = bf16[512,384]{1,0:T(8,128)(2,1)S(1)} collective-permute-done((bf16[512,384]{1,0:T(8,128)(2,1)}, bf16[512,384]{1,0:T(8,128)(2,1)S(1)}, u32[]{:S(2)}, u32[]{:S(2)}) %collective-permute-start.4) | collective-permute-done | bytes 393248 | tf_op jit(solution)/shard_map/ppermute | solution.py:39
  34.6 4.3 collective-permute-start.1
  42.4 8.2 %collective-permute-done = bf16[768,384]{1,0:T(8,128)(2,1)S(1)} collective-permute-done((bf16[768,384]{1,0:T(8,128)(2,1)}, bf16[768,384]{1,0:T(8,128)(2,1)S(1)}, u32[]{:S(2)}, u32[]{:S(2)}) %collective-permute-start) | collective-permute-done | bytes 589856 | tf_op jit(solution)/shard_map/ppermute | solution.py:39
  50.6 25.1 %collective-permute-done.1 = bf16[768,384]{1,0:T(8,128)(2,1)S(1)} collective-permute-done((bf16[768,384]{1,0:T(8,128)(2,1)}, bf16[768,384]{1,0:T(8,128)(2,1)S(1)}, u32[]{:S(2)}, u32[]{:S(2)}) %collective-permute-start.1) | collective-permute-done | bytes 589856 | tf_op jit(solution)/shard_map/ppermute | solution.py:39
  75.7 12.6 %collective-permute-done.2 = bf16[768,384]{1,0:T(8,128)(2,1)S(1)} collective-permute-done((bf16[768,384]{1,0:T(8,128)(2,1)}, bf16[768,384]{1,0:T(8,128)(2,1)S(1)}, u32[]{:S(2)}, u32[]{:S(2)}) %collective-permute-start.2) | collective-permute-done | bytes 589856 | tf_op jit(solution)/shard_map/ppermute | solution.py:39
  92.1 48.9 %collective-permute-done.3 = bf16[768,1536]{1,0:T(8,128)(2,1)S(1)} collective-permute-done((bf16[768,1536]{1,0:T(8,128)(2,1)S(1)}, bf16[768,1536]{1,0:T(8,128)(2,1)S(1)}, u32[]{:S(2)}, u32[]{:S(2)}) %collective-permute-start.3) | collective-permute-done | bytes 2359328 | tf_op jit(solution)/shard_map/ppermute | solution.py:39
  144.6 30.2 %collective-permute-done.9 = bf16[512,1536]{1,0:T(8,128)(2,1)} collective-permute-done((bf16[512,1536]{1,0:T(8,128)(2,1)S(1)}, bf16[512,1536]{1,0:T(8,128)(2,1)}, u32[]{:S(2)}, u32[]{:S(2)}) %collective-permute-start.9) | collective-permute-done | bytes 1572896 | tf_op jit(solution)/shard_map/ppermute | solution.py:39
  174.8 19.9 %fusion.4 = f32[3072,3072]{1,0:T(8,128)} fusion(bf16[512,1536]{1,0:T(8,128)(2,1)} %copy-done.18, bf16[512,1536]{1,0:T(8,128)(2,1)} %bitcast.14, bf16[512,1536]{1,0:T(8,128)(2,1)} %collective-permute-done.9, bf16[512,1536]{1,0:T(8,128)(2,1)} %bitcast.11), kind=kOutput, calls=%fused_computation.24 | convolution fusion | flops 9676259328 | bytes 44040192 | tf_op jit(solution)/shard_map/dot_general | solution.py:63
  194.7 37.6 %fusion = f32[768,3072]{1,0:T(8,128)} fusion(bf16[768,3072]{1,0:T(8,128)(2,1)} %copy-done.16, f32[3072,3072]{1,0:T(8,128)} %fusion.4, bf16[512,1536]{1,0:T(8,128)(2,1)} %copy-done.18, bf16[512,1536]{1,0:T(8,128)(2,1)S(1)} %bitcast.15, bf16[512,1536]{1,0:T(8,128)(2,1)} %collective-permute-done.9, bf16[512,1536]{1,0:T(8,128)(2,1)S(1)} %bitcast.12), kind=kOutput, calls=%fused_computation.1 | convolution fusion | flops 24225251328 | bytes 58195968 | tf_op jit(solution)/shard_map/dot_general | solution.py:63
  239.4 5.2 collective-permute-start.15
  249.5 6.1 %constant_dynamic-update-slice_fusion.6 = (bf16[1536,1536]{1,0:T(8,128)(2,1)}, bf16[768,1536]{1,0:T(8,128)(2,1)}) fusion(bf16[1536,1536]{1,0:T(8,128)(2,1)} %broadcast_in_dim.3, s32[]{:T(128)S(6)} %select_n.180, bf16[768,1536]{1,0:T(8,128)(2,1)} %collective-permute-done.11, f32[768,3072]{1,0:T(8,128)} %fusion), kind=kLoop, calls=%fused_computation.71 | loop fusion | flops 3538944 | bytes 11796484 | tf_op jit(solution)/shard_map/dynamic_update_slice | solution.py:107
  256.5 8.9 %collective-permute-done.13 = bf16[768,384]{1,0:T(8,128)(2,1)} collective-permute-done((bf16[768,384]{1,0:T(8,128)(2,1)}, bf16[768,384]{1,0:T(8,128)(2,1)}, u32[]{:S(2)}, u32[]{:S(2)}) %collective-permute-start.13) | collective-permute-done | bytes 589856 | tf_op jit(solution)/shard_map/ppermute | solution.py:39
  265.4 6.7 %collective-permute-start.21 = (bf16[768,384]{1,0:T(8,128)(2,1)}, bf16[768,384]{1,0:T(8,128)(2,1)}, u32[]{:S(2)}, u32[]{:S(2)}) collective-permute-start(bf16[768,384]{1,0:T(8,128)(2,1)} %get-tuple-element.10), channel_id=1, source_target_pairs={{4,0},{5,1},{6,2},{7,3},{8,4},{9,5},{10,6},{11,7},{12,8},{13,9},{1... | collective-permute-start | bytes 1769480 | tf_op jit(solution)/shard_map/ppermute | solution.py:39
  272.1 31.2 %collective-permute-done.19 = bf16[768,384]{1,0:T(8,128)(2,1)} collective-permute-done((bf16[768,384]{1,0:T(8,128)(2,1)}, bf16[768,384]{1,0:T(8,128)(2,1)}, u32[]{:S(2)}, u32[]{:S(2)}) %collective-permute-start.19) | collective-permute-done | bytes 589856 | tf_op jit(solution)/shard_map/ppermute | solution.py:39
  303.3 4.4 collective-permute-start.22
  310.2 34.3 %collective-permute-done.21 = bf16[768,384]{1,0:T(8,128)(2,1)} collective-permute-done((bf16[768,384]{1,0:T(8,128)(2,1)}, bf16[768,384]{1,0:T(8,128)(2,1)}, u32[]{:S(2)}, u32[]{:S(2)}) %collective-permute-start.21) | collective-permute-done | bytes 589856 | tf_op jit(solution)/shard_map/ppermute | solution.py:39
  346.4 3.4 collective-permute-start.28
  349.8 8.3 %collective-permute-done.25 = bf16[768,384]{1,0:T(8,128)(2,1)} collective-permute-done((bf16[768,384]{1,0:T(8,128)(2,1)S(1)}, bf16[768,384]{1,0:T(8,128)(2,1)}, u32[]{:S(2)}, u32[]{:S(2)}) %collective-permute-start.25) | collective-permute-done | bytes 589856 | tf_op jit(solution)/shard_map/ppermute | solution.py:39
  361.1 9.8 %collective-permute-done.31 = bf16[768,384]{1,0:T(8,128)(2,1)} collective-permute-done((bf16[768,384]{1,0:T(8,128)(2,1)}, bf16[768,384]{1,0:T(8,128)(2,1)}, u32[]{:S(2)}, u32[]{:S(2)}) %collective-permute-start.31) | collective-permute-done | bytes 589856 | tf_op jit(solution)/shard_map/ppermute | solution.py:39
  373.7 8.7 %collective-permute-done.27 = bf16[768,384]{1,0:T(8,128)(2,1)} collective-permute-done((bf16[768,384]{1,0:T(8,128)(2,1)S(1)}, bf16[768,384]{1,0:T(8,128)(2,1)}, u32[]{:S(2)}, u32[]{:S(2)}) %collective-permute-start.27) | collective-permute-done | bytes 589856 | tf_op jit(solution)/shard_map/ppermute | solution.py:39
  387.7 6.3 %collective-permute-done.14 = bf16[768,384]{1,0:T(8,128)(2,1)} collective-permute-done((bf16[768,384]{1,0:T(8,128)(2,1)}, bf16[768,384]{1,0:T(8,128)(2,1)}, u32[]{:S(2)}, u32[]{:S(2)}) %collective-permute-start.14) | collective-permute-done | bytes 589856 | tf_op jit(solution)/shard_map/ppermute | solution.py:56
  394.0 4.9 collective-permute-start.26
  398.9 7.7 %collective-permute-done.20 = bf16[768,384]{1,0:T(8,128)(2,1)} collective-permute-done((bf16[768,384]{1,0:T(8,128)(2,1)}, bf16[768,384]{1,0:T(8,128)(2,1)}, u32[]{:S(2)}, u32[]{:S(2)}) %collective-permute-start.20) | collective-permute-done | bytes 589856 | tf_op jit(solution)/shard_map/ppermute | solution.py:56
  406.6 4.9 collective-permute-start.32
  413.6 5.7 %collective-permute-done.33 = bf16[768,384]{1,0:T(8,128)(2,1)} collective-permute-done((bf16[768,384]{1,0:T(8,128)(2,1)}, bf16[768,384]{1,0:T(8,128)(2,1)}, u32[]{:S(2)}, u32[]{:S(2)}) %collective-permute-start.33) | collective-permute-done | bytes 589856 | tf_op jit(solution)/shard_map/ppermute | solution.py:39
  419.3 12.6 %collective-permute-done.26 = bf16[768,384]{1,0:T(8,128)(2,1)} collective-permute-done((bf16[768,384]{1,0:T(8,128)(2,1)}, bf16[768,384]{1,0:T(8,128)(2,1)}, u32[]{:S(2)}, u32[]{:S(2)}) %collective-permute-start.26) | collective-permute-done | bytes 589856 | tf_op jit(solution)/shard_map/ppermute | solution.py:56
  431.9 12.6 %collective-permute-done.32 = bf16[768,384]{1,0:T(8,128)(2,1)} collective-permute-done((bf16[768,384]{1,0:T(8,128)(2,1)}, bf16[768,384]{1,0:T(8,128)(2,1)}, u32[]{:S(2)}, u32[]{:S(2)}) %collective-permute-start.32) | collective-permute-done | bytes 589856 | tf_op jit(solution)/shard_map/ppermute | solution.py:56
  483.3 12.5 %collective-permute-done.24 = bf16[384,768]{0,1:T(8,128)(2,1)S(1)} collective-permute-done((bf16[384,768]{0,1:T(8,128)(2,1)S(1)}, bf16[384,768]{0,1:T(8,128)(2,1)S(1)}, u32[]{:S(2)}, u32[]{:S(2)}) %collective-permute-start.24) | collective-permute-done | bytes 589856 | tf_op jit(solution)/shard_map/ppermute | solution.py:39
  495.9 12.5 %collective-permute-done.30 = bf16[384,768]{0,1:T(8,128)(2,1)S(1)} collective-permute-done((bf16[384,768]{0,1:T(8,128)(2,1)S(1)}, bf16[384,768]{0,1:T(8,128)(2,1)S(1)}, u32[]{:S(2)}, u32[]{:S(2)}) %collective-permute-start.30) | collective-permute-done | bytes 589856 | tf_op jit(solution)/shard_map/ppermute | solution.py:39
  508.6 12.5 %collective-permute-done.36 = bf16[384,768]{0,1:T(8,128)(2,1)S(1)} collective-permute-done((bf16[384,768]{0,1:T(8,128)(2,1)S(1)}, bf16[384,768]{0,1:T(8,128)(2,1)S(1)}, u32[]{:S(2)}, u32[]{:S(2)}) %collective-permute-start.36) | collective-permute-done | bytes 589856 | tf_op jit(solution)/shard_map/ppermute | solution.py:39
  522.9 4.4 copy.9
  (126 shorter events, 99.8 us)
Async XLA Ops:
  8.8 19.8 %collective-permute-start.4 = (bf16[512,384]{1,0:T(8,128)(2,1)}, bf16[512,384]{1,0:T(8,128)(2,1)S(1)}, u32[]{:S(2)}, u32[]{:S(2)}) collective-permute-start(bf16[512,384]{1,0:T(8,128)(2,1)} %pad_maximum_fusion.26), channel_id=1, source_target_pairs={{8,0},{9,1},{10,2},{11,3},{12,4},{13,5},{14,6},{15,7},{0,8},{1,9},... | collective-permute-start | bytes 1179656 | tf_op jit(solution)/shard_map/ppermute | solution.py:39
  11.1 27.8 %collective-permute-start.6 = (bf16[512,384]{1,0:T(8,128)(2,1)}, bf16[512,384]{1,0:T(8,128)(2,1)S(1)}, u32[]{:S(2)}, u32[]{:S(2)}) collective-permute-start(bf16[512,384]{1,0:T(8,128)(2,1)} %pad_maximum_fusion.26), channel_id=1, source_target_pairs={{4,0},{5,1},{6,2},{7,3},{8,4},{9,5},{10,6},{11,7},{12,8},{13,9},{1... | collective-permute-start | bytes 1179656 | tf_op jit(solution)/shard_map/ppermute | solution.py:39
  13.2 26.5 %collective-permute-start.7 = (bf16[512,384]{1,0:T(8,128)(2,1)}, bf16[512,384]{1,0:T(8,128)(2,1)}, u32[]{:S(2)}, u32[]{:S(2)}) collective-permute-start(bf16[512,384]{1,0:T(8,128)(2,1)} %pad_maximum_fusion.26), channel_id=1, source_target_pairs={{0,4},{1,5},{2,6},{3,7},{4,8},{5,9},{6,10},{7,11},{8,12},{9,13},{1... | collective-permute-start | bytes 1179656 | tf_op jit(solution)/shard_map/ppermute | solution.py:39
  34.6 16.0 %collective-permute-start = (bf16[768,384]{1,0:T(8,128)(2,1)}, bf16[768,384]{1,0:T(8,128)(2,1)S(1)}, u32[]{:S(2)}, u32[]{:S(2)}) collective-permute-start(bf16[768,384]{1,0:T(8,128)(2,1)} %get-tuple-element.19), channel_id=1, source_target_pairs={{4,0},{5,1},{6,2},{7,3},{8,4},{9,5},{10,6},{11,7},{12,8},{13,9},{1... | collective-permute-start | bytes 1769480 | tf_op jit(solution)/shard_map/ppermute | solution.py:39
  34.6 41.1 %collective-permute-start.1 = (bf16[768,384]{1,0:T(8,128)(2,1)}, bf16[768,384]{1,0:T(8,128)(2,1)S(1)}, u32[]{:S(2)}, u32[]{:S(2)}) collective-permute-start(bf16[768,384]{1,0:T(8,128)(2,1)} %get-tuple-element.18), channel_id=1, source_target_pairs={{8,0},{9,1},{10,2},{11,3},{12,4},{13,5},{14,6},{15,7},{0,8},{1,9},... | collective-permute-start | bytes 1769480 | tf_op jit(solution)/shard_map/ppermute | solution.py:39
  39.6 48.7 %collective-permute-start.2 = (bf16[768,384]{1,0:T(8,128)(2,1)}, bf16[768,384]{1,0:T(8,128)(2,1)S(1)}, u32[]{:S(2)}, u32[]{:S(2)}) collective-permute-start(bf16[768,384]{1,0:T(8,128)(2,1)} %get-tuple-element.17), channel_id=1, source_target_pairs={{12,0},{13,1},{14,2},{15,3},{0,4},{1,5},{2,6},{3,7},{4,8},{5,9},{6... | collective-permute-start | bytes 1769480 | tf_op jit(solution)/shard_map/ppermute | solution.py:39
  41.1 48.9 %collective-permute-start.8 = (bf16[512,1536]{1,0:T(8,128)(2,1)S(1)}, bf16[512,1536]{1,0:T(8,128)(2,1)S(1)}, u32[]{:S(2)}, u32[]{:S(2)}) collective-permute-start(bf16[512,1536]{1,0:T(8,128)(2,1)S(1)} %pad_maximum_fusion.17), channel_id=1, source_target_pairs={{16,0},{0,16},{17,1},{1,17},{18,2},{2,18},{19,3},{3,19},{20,4},{4,... | collective-permute-start | bytes 4718600 | tf_op jit(solution)/shard_map/ppermute | solution.py:39
  88.6 52.4 %collective-permute-start.3 = (bf16[768,1536]{1,0:T(8,128)(2,1)S(1)}, bf16[768,1536]{1,0:T(8,128)(2,1)S(1)}, u32[]{:S(2)}, u32[]{:S(2)}) collective-permute-start(bf16[768,1536]{1,0:T(8,128)(2,1)S(1)} %pad_maximum_fusion.2), channel_id=1, source_target_pairs={{2,0},{3,1},{0,2},{1,3},{6,4},{7,5},{4,6},{5,7},{10,8},{11,9},{8,1... | collective-permute-start | bytes 7077896 | tf_op jit(solution)/shard_map/ppermute | solution.py:39
  90.3 51.0 %collective-permute-start.10 = (bf16[512,1536]{1,0:T(8,128)(2,1)S(1)}, bf16[512,1536]{1,0:T(8,128)(2,1)S(1)}, u32[]{:S(2)}, u32[]{:S(2)}) collective-permute-start(bf16[512,1536]{1,0:T(8,128)(2,1)S(1)} %bitcast.13), channel_id=1, source_target_pairs={{1,0},{0,1},{3,2},{2,3},{5,4},{4,5},{7,6},{6,7},{9,8},{8,9},{11,10... | collective-permute-start | bytes 4718600 | tf_op jit(solution)/shard_map/ppermute | solution.py:39
  91.2 83.6 %collective-permute-start.9 = (bf16[512,1536]{1,0:T(8,128)(2,1)S(1)}, bf16[512,1536]{1,0:T(8,128)(2,1)}, u32[]{:S(2)}, u32[]{:S(2)}) collective-permute-start(bf16[512,1536]{1,0:T(8,128)(2,1)S(1)} %bitcast.10), channel_id=1, source_target_pairs={{2,0},{3,1},{0,2},{1,3},{6,4},{7,5},{4,6},{5,7},{10,8},{11,9},{8,1... | collective-permute-start | bytes 4718600 | tf_op jit(solution)/shard_map/ppermute | solution.py:39
  239.4 25.9 %collective-permute-start.13 = (bf16[768,384]{1,0:T(8,128)(2,1)}, bf16[768,384]{1,0:T(8,128)(2,1)}, u32[]{:S(2)}, u32[]{:S(2)}) collective-permute-start(bf16[768,384]{1,0:T(8,128)(2,1)} %get-tuple-element.9), channel_id=1, source_target_pairs={{8,0},{9,1},{10,2},{11,3},{12,4},{13,5},{14,6},{15,7},{0,8},{1,9},... | collective-permute-start | bytes 1769480 | tf_op jit(solution)/shard_map/ppermute | solution.py:39
  239.4 68.3 %collective-permute-start.15 = (bf16[768,384]{1,0:T(8,128)(2,1)}, bf16[768,384]{1,0:T(8,128)(2,1)S(1)}, u32[]{:S(2)}, u32[]{:S(2)}) collective-permute-start(bf16[768,384]{1,0:T(8,128)(2,1)} %get-tuple-element.9), channel_id=1, source_target_pairs={{4,0},{5,1},{6,2},{7,3},{8,4},{9,5},{10,6},{11,7},{12,8},{13,9},{1... | collective-permute-start | bytes 1769480 | tf_op jit(solution)/shard_map/ppermute | solution.py:39
  244.6 63.2 %collective-permute-start.16 = (bf16[768,384]{1,0:T(8,128)(2,1)}, bf16[768,384]{1,0:T(8,128)(2,1)}, u32[]{:S(2)}, u32[]{:S(2)}) collective-permute-start(bf16[768,384]{1,0:T(8,128)(2,1)} %get-tuple-element.9), channel_id=1, source_target_pairs={{0,4},{1,5},{2,6},{3,7},{4,8},{5,9},{6,10},{7,11},{8,12},{9,13},{1... | collective-permute-start | bytes 1769480 | tf_op jit(solution)/shard_map/ppermute | solution.py:39
  246.6 56.7 %collective-permute-start.19 = (bf16[768,384]{1,0:T(8,128)(2,1)}, bf16[768,384]{1,0:T(8,128)(2,1)}, u32[]{:S(2)}, u32[]{:S(2)}) collective-permute-start(bf16[768,384]{1,0:T(8,128)(2,1)} %get-tuple-element.10), channel_id=1, source_target_pairs={{8,0},{9,1},{10,2},{11,3},{12,4},{13,5},{14,6},{15,7},{0,8},{1,9},... | collective-permute-start | bytes 1769480 | tf_op jit(solution)/shard_map/ppermute | solution.py:39
  255.5 191.2 %collective-permute-start.12 = (bf16[768,1536]{1,0:T(8,128)(2,1)}, bf16[768,1536]{1,0:T(8,128)(2,1)S(1)}, u32[]{:S(2)}, u32[]{:S(2)}) collective-permute-start(bf16[768,1536]{1,0:T(8,128)(2,1)} %get-tuple-element.6), channel_id=1, source_target_pairs={{16,0},{0,16},{17,1},{1,17},{18,2},{2,18},{19,3},{3,19},{20,4},{4,... | collective-permute-start | bytes 7077896 | tf_op jit(solution)/shard_map/ppermute | solution.py:39
  265.4 79.1 %collective-permute-start.21 = (bf16[768,384]{1,0:T(8,128)(2,1)}, bf16[768,384]{1,0:T(8,128)(2,1)}, u32[]{:S(2)}, u32[]{:S(2)}) collective-permute-start(bf16[768,384]{1,0:T(8,128)(2,1)} %get-tuple-element.10), channel_id=1, source_target_pairs={{4,0},{5,1},{6,2},{7,3},{8,4},{9,5},{10,6},{11,7},{12,8},{13,9},{1... | collective-permute-start | bytes 1769480 | tf_op jit(solution)/shard_map/ppermute | solution.py:39
  303.3 43.1 %collective-permute-start.22 = (bf16[768,384]{1,0:T(8,128)(2,1)}, bf16[768,384]{1,0:T(8,128)(2,1)}, u32[]{:S(2)}, u32[]{:S(2)}) collective-permute-start(bf16[768,384]{1,0:T(8,128)(2,1)} %get-tuple-element.10), channel_id=1, source_target_pairs={{0,4},{1,5},{2,6},{3,7},{4,8},{5,9},{6,10},{7,11},{8,12},{9,13},{1... | collective-permute-start | bytes 1769480 | tf_op jit(solution)/shard_map/ppermute | solution.py:39
  307.8 50.4 %collective-permute-start.25 = (bf16[768,384]{1,0:T(8,128)(2,1)S(1)}, bf16[768,384]{1,0:T(8,128)(2,1)}, u32[]{:S(2)}, u32[]{:S(2)}) collective-permute-start(bf16[768,384]{1,0:T(8,128)(2,1)S(1)} %copy-done.13), channel_id=1, source_target_pairs={{8,0},{9,1},{10,2},{11,3},{12,4},{13,5},{14,6},{15,7},{0,8},{1,9},... | collective-permute-start | bytes 1769480 | tf_op jit(solution)/shard_map/ppermute | solution.py:39
  307.8 63.0 %collective-permute-start.31 = (bf16[768,384]{1,0:T(8,128)(2,1)}, bf16[768,384]{1,0:T(8,128)(2,1)}, u32[]{:S(2)}, u32[]{:S(2)}) collective-permute-start(bf16[768,384]{1,0:T(8,128)(2,1)} %get-tuple-element.11), channel_id=1, source_target_pairs={{8,0},{9,1},{10,2},{11,3},{12,4},{13,5},{14,6},{15,7},{0,8},{1,9},... | collective-permute-start | bytes 1769480 | tf_op jit(solution)/shard_map/ppermute | solution.py:39
  344.5 38.0 %collective-permute-start.27 = (bf16[768,384]{1,0:T(8,128)(2,1)S(1)}, bf16[768,384]{1,0:T(8,128)(2,1)}, u32[]{:S(2)}, u32[]{:S(2)}) collective-permute-start(bf16[768,384]{1,0:T(8,128)(2,1)S(1)} %copy-done.13), channel_id=1, source_target_pairs={{4,0},{5,1},{6,2},{7,3},{8,4},{9,5},{10,6},{11,7},{12,8},{13,9},{1... | collective-permute-start | bytes 1769480 | tf_op jit(solution)/shard_map/ppermute | solution.py:39
  346.4 39.1 %collective-permute-start.28 = (bf16[768,384]{1,0:T(8,128)(2,1)S(1)}, bf16[768,384]{1,0:T(8,128)(2,1)}, u32[]{:S(2)}, u32[]{:S(2)}) collective-permute-start(bf16[768,384]{1,0:T(8,128)(2,1)S(1)} %copy-done.13), channel_id=1, source_target_pairs={{0,4},{1,5},{2,6},{3,7},{4,8},{5,9},{6,10},{7,11},{8,12},{9,13},{1... | collective-permute-start | bytes 1769480 | tf_op jit(solution)/shard_map/ppermute | solution.py:39
  358.1 35.9 %collective-permute-start.14 = (bf16[768,384]{1,0:T(8,128)(2,1)}, bf16[768,384]{1,0:T(8,128)(2,1)}, u32[]{:S(2)}, u32[]{:S(2)}) collective-permute-start(bf16[768,384]{1,0:T(8,128)(2,1)} %collective-permute-done.13), channel_id=1, source_target_pairs={{4,0},{5,1},{6,2},{7,3},{8,12},{9,13},{10,14},{11,15},{20,16},{21,... | collective-permute-start | bytes 1769480 | tf_op jit(solution)/shard_map/ppermute | solution.py:56
  370.8 35.8 %collective-permute-start.20 = (bf16[768,384]{1,0:T(8,128)(2,1)}, bf16[768,384]{1,0:T(8,128)(2,1)}, u32[]{:S(2)}, u32[]{:S(2)}) collective-permute-start(bf16[768,384]{1,0:T(8,128)(2,1)} %collective-permute-done.19), channel_id=1, source_target_pairs={{4,0},{5,1},{6,2},{7,3},{8,12},{9,13},{10,14},{11,15},{20,16},{21,... | collective-permute-start | bytes 1769480 | tf_op jit(solution)/shard_map/ppermute | solution.py:56
  382.4 36.8 %collective-permute-start.33 = (bf16[768,384]{1,0:T(8,128)(2,1)}, bf16[768,384]{1,0:T(8,128)(2,1)}, u32[]{:S(2)}, u32[]{:S(2)}) collective-permute-start(bf16[768,384]{1,0:T(8,128)(2,1)} %get-tuple-element.11), channel_id=1, source_target_pairs={{4,0},{5,1},{6,2},{7,3},{8,4},{9,5},{10,6},{11,7},{12,8},{13,9},{1... | collective-permute-start | bytes 1769480 | tf_op jit(solution)/shard_map/ppermute | solution.py:39
  385.5 33.8 %collective-permute-start.34 = (bf16[768,384]{1,0:T(8,128)(2,1)}, bf16[768,384]{1,0:T(8,128)(2,1)}, u32[]{:S(2)}, u32[]{:S(2)}) collective-permute-start(bf16[768,384]{1,0:T(8,128)(2,1)} %get-tuple-element.11), channel_id=1, source_target_pairs={{0,4},{1,5},{2,6},{3,7},{4,8},{5,9},{6,10},{7,11},{8,12},{9,13},{1... | collective-permute-start | bytes 1769480 | tf_op jit(solution)/shard_map/ppermute | solution.py:39
  394.0 37.9 %collective-permute-start.26 = (bf16[768,384]{1,0:T(8,128)(2,1)}, bf16[768,384]{1,0:T(8,128)(2,1)}, u32[]{:S(2)}, u32[]{:S(2)}) collective-permute-start(bf16[768,384]{1,0:T(8,128)(2,1)} %collective-permute-done.25), channel_id=1, source_target_pairs={{4,0},{5,1},{6,2},{7,3},{8,12},{9,13},{10,14},{11,15},{20,16},{21,... | collective-permute-start | bytes 1769480 | tf_op jit(solution)/shard_map/ppermute | solution.py:56
  406.6 37.9 %collective-permute-start.32 = (bf16[768,384]{1,0:T(8,128)(2,1)}, bf16[768,384]{1,0:T(8,128)(2,1)}, u32[]{:S(2)}, u32[]{:S(2)}) collective-permute-start(bf16[768,384]{1,0:T(8,128)(2,1)} %collective-permute-done.31), channel_id=1, source_target_pairs={{4,0},{5,1},{6,2},{7,3},{8,12},{9,13},{10,14},{11,15},{20,16},{21,... | collective-permute-start | bytes 1769480 | tf_op jit(solution)/shard_map/ppermute | solution.py:56
  465.2 12.9 %collective-permute-start.35 = (bf16[768,768]{0,1:T(8,128)(2,1)S(1)}, bf16[768,768]{0,1:T(8,128)(2,1)S(1)}, u32[]{:S(2)}, u32[]{:S(2)}) collective-permute-start(bf16[768,768]{0,1:T(8,128)(2,1)S(1)} %convolution_convert_fusion), channel_id=1, source_target_pairs={{1,0},{0,1},{3,2},{2,3},{5,4},{4,5},{7,6},{6,7},{9,8},{8,9},{11,10... | collective-permute-start | bytes 3538952 | tf_op jit(solution)/shard_map/ppermute | solution.py:39
  468.6 14.5 %collective-permute-start.18 = (bf16[384,768]{0,1:T(8,128)(2,1)S(1)}, bf16[384,768]{0,1:T(8,128)(2,1)S(1)}, u32[]{:S(2)}, u32[]{:S(2)}) collective-permute-start(bf16[384,768]{0,1:T(8,128)(2,1)S(1)} %slice.95), channel_id=1, source_target_pairs={{2,0},{3,1},{0,2},{1,3},{6,4},{7,5},{4,6},{5,7},{10,8},{11,9},{8,1... | collective-permute-start | bytes 1769480 | tf_op jit(solution)/shard_map/ppermute | solution.py:39
  473.3 22.5 %collective-permute-start.24 = (bf16[384,768]{0,1:T(8,128)(2,1)S(1)}, bf16[384,768]{0,1:T(8,128)(2,1)S(1)}, u32[]{:S(2)}, u32[]{:S(2)}) collective-permute-start(bf16[384,768]{0,1:T(8,128)(2,1)S(1)} %slice.94), channel_id=1, source_target_pairs={{2,0},{3,1},{0,2},{1,3},{6,4},{7,5},{4,6},{5,7},{10,8},{11,9},{8,1... | collective-permute-start | bytes 1769480 | tf_op jit(solution)/shard_map/ppermute | solution.py:39
  476.8 31.7 %collective-permute-start.30 = (bf16[384,768]{0,1:T(8,128)(2,1)S(1)}, bf16[384,768]{0,1:T(8,128)(2,1)S(1)}, u32[]{:S(2)}, u32[]{:S(2)}) collective-permute-start(bf16[384,768]{0,1:T(8,128)(2,1)S(1)} %slice.93), channel_id=1, source_target_pairs={{2,0},{3,1},{0,2},{1,3},{6,4},{7,5},{4,6},{5,7},{10,8},{11,9},{8,1... | collective-permute-start | bytes 1769480 | tf_op jit(solution)/shard_map/ppermute | solution.py:39
  481.4 39.7 %collective-permute-start.36 = (bf16[384,768]{0,1:T(8,128)(2,1)S(1)}, bf16[384,768]{0,1:T(8,128)(2,1)S(1)}, u32[]{:S(2)}, u32[]{:S(2)}) collective-permute-start(bf16[384,768]{0,1:T(8,128)(2,1)S(1)} %slice.92), channel_id=1, source_target_pairs={{2,0},{3,1},{0,2},{1,3},{6,4},{7,5},{4,6},{5,7},{10,8},{11,9},{8,1... | collective-permute-start | bytes 1769480 | tf_op jit(solution)/shard_map/ppermute | solution.py:39
  (26 other events, 388.6 us)

commit v2 on v0

v2 whole, which is shorter than its diff:
```python
import jax
import jax.numpy as jnp
from jax import lax
from jax.experimental import pallas as pl
from jax.experimental.pallas import tpu as pltpu
from jax.sharding import PartitionSpec as P

damping = 0.1
pair = 2
shares = (5, 1)
f32 = jnp.float32
bf16 = jnp.bfloat16
params = pltpu.CompilerParams(vmem_limit_bytes=48 * 2**20)


def pairs(size, shift):
    return [((i + shift) % size, i) for i in range(size)]


def fetch(value, axis, shift=1):
    return lax.ppermute(value, axis, pairs(lax.axis_size(axis), shift))


def gather(value, axis):
    return [value] + [fetch(value, axis, s) for s in range(1, lax.axis_size(axis))]


def dot(a, b, contract):
    return lax.dot_general(a, b, (contract, ((), ())), preferred_element_type=f32)


def after(value, *others):
    return pl.pallas_call(
        lambda *refs: None,
        out_shape=jax.ShapeDtypeStruct(value.shape, value.dtype),
        in_specs=[pl.BlockSpec(memory_space=pl.ANY)] * (1 + len(others)),
        out_specs=pl.BlockSpec(memory_space=pl.ANY),
        input_output_aliases={0: 0},
    )(value, *others)


def square(v):
    return (v.astype(f32) ** 2).astype(bf16)


def tile(size, most):
    fits = [t for t in range(128, most + 1, 128) if size % t == 0]
    return max(fits) if fits else size


def pack(groups, others, rows):
    count, wide = len(groups), len(groups[0])
    cols = groups[0][0].shape[1]

    def body(*refs):
        left_ref, other_ref, right_ref = refs[-3:]
        for s in range(count):
            for g in range(wide):
                ref = refs[s * wide + g]
                span = slice(g * rows, (g + 1) * rows)
                left_ref[s, :, span] = ref[:rows, :].T
                right_ref[span, s * cols : (s + 1) * cols] = ref[rows:, :]
                other_ref[s, :, span] = refs[(count + s) * wide + g][...].T

    left = jax.ShapeDtypeStruct((count, cols, wide * rows), bf16)
    return pl.pallas_call(
        body,
        out_shape=[left, left, jax.ShapeDtypeStruct((wide * rows, count * cols), bf16)],
        compiler_params=params,
    )(*[v for group in groups + others for v in group])


def mix(rows, left, rights, first, part, parts, kind, carry=None):
    count, cols, tok = left.shape
    n = rows[0].shape[0]
    span = rights[0].shape[1] // parts
    tj = tile(span, 768)
    runs = span // tj
    group = 2 if count % 2 == 0 and cols % 128 == 0 else 1

    def body(first_ref, *refs):
        row_refs, left_ref, refs = refs[:count], refs[count], refs[count + 1 :]
        right_refs, out_ref = refs[: len(rights)], refs[-1]
        j = pl.program_id(0)
        b = jnp.where(j // runs == first_ref[0], right_refs[0][...], right_refs[1][...])
        b2 = square(b)
        total = refs[len(rights)][...] if carry is not None else None
        for k in range(0, count, group):
            a = left_ref[k : k + group].reshape(group * cols, tok)
            summed = jnp.dot(a, b, preferred_element_type=f32)
            moment = jnp.dot(square(a), b2, preferred_element_type=f32)
            ratio = (summed / (moment + damping * tok)).astype(bf16)
            lead = [row_refs[k + i][...] for i in range(group)]
            lead = jnp.concatenate(lead, axis=1) if group > 1 else lead[0]
            step = jnp.dot(lead, ratio, preferred_element_type=f32)
            total = step if total is None else total + step
        out_ref[...] = total.astype(kind)

    specs = [pl.BlockSpec((n, cols), lambda j, f: (0, 0)) for _ in rows]
    specs += [pl.BlockSpec((count, cols, tok), lambda j, f: (0, 0, 0))]
    specs += [pl.BlockSpec((tok, tj), lambda j, f: (0, part * runs + j % runs)) for _ in rights]
    args = [*rows, left, *rights]
    if carry is not None:
        specs.append(pl.BlockSpec((n, tj), lambda j, f: (0, j)))
        args.append(carry)
    return pl.pallas_call(
        body,
        out_shape=jax.ShapeDtypeStruct((n, span * len(rights)), kind),
        grid_spec=pltpu.PrefetchScalarGridSpec(
            num_scalar_prefetch=1,
            grid=(runs * len(rights),),
            in_specs=specs,
            out_specs=pl.BlockSpec((n, tj), lambda j, f: (0, j)),
        ),
        compiler_params=params,
    )(jnp.full((1,), first, jnp.int32), *args)


def expand(halves, pick, blocks, order, kind, extra=None):
    _, n, deep = halves[0].shape
    count, wide, cols = blocks.shape
    steps = count // len(halves)
    scalars = jnp.concatenate([order, jnp.full((1,), pick, jnp.int32)])

    def body(scalar_ref, *refs):
        lefts, rights = refs[: len(halves)], refs[len(halves) : 2 * len(halves)]
        out_ref, total = refs[-2:]
        k = pl.program_id(0)
        if cols % 128 == 0:
            left = jnp.concatenate([r[0] for r in lefts], axis=1)
            right = jnp.concatenate([r[0] for r in rights], axis=1)
            step = dot(left, right, ((1,), (1,)))
        else:
            step = sum(dot(a[0, 0], b[0], ((1,), (1,))) for a, b in zip(lefts, rights))

        @pl.when(k == 0)
        def _():
            total[...] = step + refs[2 * len(halves)][...].astype(f32) if extra is not None else step

        @pl.when(k > 0)
        def _():
            total[...] += step

        @pl.when(k == steps - 1)
        def _():
            out_ref[...] = total[...].astype(kind)

    if cols % 128 == 0:
        specs = [pl.BlockSpec((1, n, cols), lambda k, s: (s[count], 0, k)) for _ in halves]
    else:
        halves = [h.reshape(h.shape[0], n, steps, cols).transpose(0, 2, 1, 3) for h in halves]
        specs = [pl.BlockSpec((1, 1, n, cols), lambda k, s: (s[count], k, 0, 0)) for _ in halves]
    for h in range(len(halves)):
        specs.append(pl.BlockSpec((1, wide, cols), lambda k, s, h=h: (s[h * steps + k], 0, 0)))
    args = [*halves, *[blocks] * len(halves)]
    if extra is not None:
        specs.append(pl.BlockSpec((n, wide), lambda k, s: (0, 0)))
        args.append(extra)
    return pl.pallas_call(
        body,
        out_shape=jax.ShapeDtypeStruct((n, wide), kind),
        grid_spec=pltpu.PrefetchScalarGridSpec(
            num_scalar_prefetch=1,
            grid=(steps,),
            in_specs=specs,
            out_specs=pl.BlockSpec((n, wide), lambda k, s: (0, 0)),
            scratch_shapes=[pltpu.VMEM((n, wide), f32)],
        ),
        compiler_params=params,
    )(scalars, *args)


def shards(tokens, out_grads, basis_in, basis_out):
    at = {k: lax.axis_index(k) for k in "yzxc"}
    nz, ny = lax.axis_size("z"), lax.axis_size("y")
    width, cols = basis_in.shape
    rows = tokens.shape[0]
    quarter = width // nz
    eighth = quarter // ny

    proj_in = jnp.dot(tokens, basis_in, preferred_element_type=f32).astype(bf16)
    proj_out = jnp.dot(out_grads, basis_out, preferred_element_type=f32).astype(bf16)
    both = jnp.concatenate([proj_in, proj_out], axis=0)
    order = [0] + sorted(range(1, nz), key=lambda s: -min(s, nz - s))
    groups, others, links = {}, {}, []
    for s in order:
        value = fetch(both, "z", s) if s else both
        links += [value] if s else []
        groups[s] = gather(value, "y")
        others[s] = gather(fetch(value[:rows], "x"), "y")
    every = range(nz)
    left, left_other, right = pack([groups[s] for s in every], [others[s] for s in every], rows)
    rights = [right, fetch(right, "c")]

    blocks = pair * pair
    share = quarter // (blocks * ny)
    in_view = basis_in.reshape(nz, blocks, ny, share, cols)
    in_own, in_other = {}, {}
    for s in order:
        to = (at["z"] + nz - s) % nz
        block = lax.dynamic_slice(in_view, (to, 0, at["y"], 0, 0), (1, blocks, 1, share, cols))
        block = block.reshape(eighth, cols)
        in_own[s] = fetch(after(block, *links, in_other[0]), "z", s) if s else block
        in_other[s] = fetch(in_own[s], "x")
    in_own = [in_own[s] for s in range(nz)]
    in_other = [in_other[s] for s in range(nz)]

    out_rows = width // ny
    cuts = [out_rows * sum(shares[:k]) // sum(shares) // 128 * 128 for k in range(len(shares))] + [out_rows]
    sizes = [b - a for a, b in zip(cuts, cuts[1:])]
    wides, gate = [], [*in_own[1:], left]
    for k in range(len(shares)):
        first = at["y"] * out_rows + cuts[k]
        raw = lax.dynamic_slice_in_dim(basis_out, first, sizes[k], 0)
        raw = after(raw, *gate) if gate else raw
        wides.append(lax.all_gather(raw, ("z", "c"), axis=0))

    parts = [mix(in_own, left, rights, at["c"], h, 2, f32) for h in range(2)]
    halves = []
    take = lambda v, axis, i: lax.dynamic_index_in_dim(v, i, axis, keepdims=False)
    for h in range(2):
        ready = after(left_other, mine) if h else left_other
        part = mix(in_other, ready, rights, at["c"], h, 2, bf16, parts[h])
        view = part.reshape(pair, pair, share, -1)
        away = fetch(take(view, 1, 1 - at["c"]), "c")
        mine = (take(view, 1, at["c"]).astype(f32) + away.astype(f32)).astype(bf16)
        got = gather(mine, "y")
        full = jnp.stack(
            [lax.select_n((ny + j - at["y"]) % ny, *got) if ny > 2 else
             jnp.where(at["y"] == j, got[0], got[-1]) for j in range(ny)], axis=1)
        halves.append(full.reshape(pair, ny * share, -1))
    place = [
        ((at["z"] + h * (nz // 2) + s) % nz) * pair + j
        for h in range(2) for j in range(pair) for s in range(nz // 2)
    ]
    place = jnp.stack(place).astype(jnp.int32)

    done = []
    for k in range(len(shares)):
        wide = after(wides[k], kept) if k else wides[k]
        given = fetch(expand(halves, 1 - at["x"], wide, place, bf16), "x")
        kept = expand(halves, at["x"], wide, place, f32)
        done.append((kept + given.astype(f32)).astype(bf16))
    return jnp.concatenate(done, axis=1)


def solution(mesh):
    sizes = (mesh.shape["dp"], mesh.shape["panel"] // (pair * pair), pair, pair)
    grid = jax.sharding.Mesh(mesh.devices.reshape(sizes), ("y", "z", "x", "c"))
    panels = ("z", "x", "c")
    return jax.shard_map(
        shards,
        mesh=grid,
        in_specs=(P("y", None), P("y", None), P(None, panels), P(None, panels)),
        out_specs=P(panels, "y"),
        check_vma=False,
    )
```

time: 805 us -> 352 us (0.44)
  waiting for transfers between devices: 543 us -> 164 us
  blocking collectives: 158 us -> 0 us
  Pallas kernels: 0 us -> 94.2 us
  matrix products: 62.3 us -> 6.08 us
  starting transfers between devices: 0.35 us -> 26.2 us
  local copies, waits for them, and re-layouts: 16.4 us -> 31.3 us
    all_gather x4 -> x2, waiting for transfers between devices: 432 us -> 0.01 us  [shards(): wides.append(lax.all_gather(raw, ('z', 'c'), axis=0))]
    ppermute x0 -> x29, waiting for transfers between devices: none -> 164 us  [fetch(): return lax.ppermute(value, axis, pairs(lax.axis_size(axis), shift))]
    all_to_all x1 -> x0, blocking collectives: 158 us -> none  [shards(): lax.all_to_all(basis_in, 'panel', split_axis=0, concat_axis=1, tiled=True)]
    reduce_scatter x1 -> x0, waiting for transfers between devices: 110 us -> none  [shards(): lax.psum_scatter(partials.astype(jnp.bfloat16), 'dp', scatter_dimension=2...]
    pallas_call x0 -> x16, Pallas kernels: none -> 94.2 us  [the longest x4 53.2 us: mix(): pl.pallas_call(body, out_shape=jax.ShapeDtypeStruct((n, span * len(rights...]
    dot_general x6 -> x2, matrix products: 62.3 us -> 6.08 us  [the longest x1 4.28 us: shards(): proj_in = jnp.dot(tokens, basis_in, preferred_element_type=f32).astype(bf16)]
    ppermute x0 -> x29, starting transfers between devices: none -> 25.9 us  [fetch(): return lax.ppermute(value, axis, pairs(lax.axis_size(axis), shift))]
    unnamed x6 -> x76, local copies, waits for them, and re-layouts: 2.16 us -> 17.8 us
  transfers between devices with their start and end apart: 5 -> 31, of which waited for: 5 -> 19; matrix products, arithmetic and copies ran while one was open for 2% -> 6% of each run, Pallas kernels for 0% -> 27%
where the time goes in v2:
time: 352 us; the launch traced here: 349 us
  waiting for transfers between devices  164 us (47%)
  Pallas kernels  94.2 us (27%)
  local copies, waits for them, and re-layouts  31.3 us (9%)
  starting transfers between devices  26.2 us (7%)
  between operations  13.7 us (4%)
  other arithmetic  13 us (4%)
  matrix products  6.08 us (2%)
    ppermute x29, waiting for transfers between devices, fetch(): return lax.ppermute(value, axis, pairs(lax.axis_size(axis), shift))  164 us
    pallas_call x4, Pallas kernels, mix(): pl.pallas_call(body, out_shape=jax.ShapeDtypeStruct((n, span * len(rights...  53.2 us
    pallas_call x4, Pallas kernels, expand(): pl.pallas_call(body, out_shape=jax.ShapeDtypeStruct((n, wide), kind), gri...  36.9 us
    ppermute x29, starting transfers between devices, fetch(): return lax.ppermute(value, axis, pairs(lax.axis_size(axis), shift))  25.9 us
    unnamed x76, local copies, waits for them, and re-layouts  17.8 us
  transfers between devices with their start and end apart: 31, of which 19 were waited for; matrix products, arithmetic and copies ran while one was open for 6% of the time, Pallas kernels for 27%

profile of v2, /device:TPU:9, one launch (start us, length us, event | category | flops | bytes accessed | tf_op | source)
XLA Modules:
  0.0 348.8 jit_solution(14939890454451398617)
XLA Ops:
  8.4 4.3 %convolution_convert_fusion.1 = bf16[256,384]{1,0:T(8,128)(2,1)S(1)} fusion(bf16[256,6144]{1,0:T(8,128)(2,1)S(1)} %copy-done, bf16[6144,384]{1,0:T(8,128)(2,1)} %param.6), kind=kOutput, calls=%fused_computation.15 | convolution fusion | flops 1208057856 | bytes 8060928 | tf_op jit(solution)/shard_map/dot_general | solution.py:181
  15.0 2.4 collective-permute-start.1
  17.6 2.9 constant_dynamic-slice_fusion.2
  25.1 25.5 %collective-permute-done.2.refs_2_ = bf16[512,384]{1,0:T(8,128)(2,1)S(1)} collective-permute-done((bf16[512,384]{1,0:T(8,128)(2,1)S(1)}, bf16[512,384]{1,0:T(8,128)(2,1)S(1)}, u32[]{:S(2)}, u32[]{:S(2)}) %collective-permute-start.2) | collective-permute-done | bytes 393248 | tf_op jit(solution)/shard_map/ppermute | solution.py:21
  53.3 2.5 collective-permute-done.14.refs_8_
  60.7 3.6 %collective-permute-done.18.refs_12_ = bf16[256,384]{1,0:T(8,128)(2,1)} collective-permute-done((bf16[256,384]{1,0:T(8,128)(2,1)S(1)}, bf16[256,384]{1,0:T(8,128)(2,1)}, u32[]{:S(2)}, u32[]{:S(2)}) %collective-permute-start.18) | collective-permute-done | bytes 196640 | tf_op jit(solution)/shard_map/ppermute | solution.py:21
  65.0 3.5 %collective-permute-done.20.refs_14_ = bf16[256,384]{1,0:T(8,128)(2,1)} collective-permute-done((bf16[256,384]{1,0:T(8,128)(2,1)S(1)}, bf16[256,384]{1,0:T(8,128)(2,1)}, u32[]{:S(2)}, u32[]{:S(2)}) %collective-permute-start.20) | collective-permute-done | bytes 196640 | tf_op jit(solution)/shard_map/ppermute | solution.py:21
  72.1 3.5 %collective-permute-done.19.refs_13_ = bf16[256,384]{1,0:T(8,128)(2,1)S(1)} collective-permute-done((bf16[256,384]{1,0:T(8,128)(2,1)}, bf16[256,384]{1,0:T(8,128)(2,1)S(1)}, u32[]{:S(2)}, u32[]{:S(2)}) %collective-permute-start.19) | collective-permute-done | bytes 196640 | tf_op jit(solution)/shard_map/ppermute | solution.py:21
  76.3 3.5 %collective-permute-done.21.refs_15_ = bf16[256,384]{1,0:T(8,128)(2,1)} collective-permute-done((bf16[256,384]{1,0:T(8,128)(2,1)}, bf16[256,384]{1,0:T(8,128)(2,1)}, u32[]{:S(2)}, u32[]{:S(2)}) %collective-permute-start.21) | collective-permute-done | bytes 196640 | tf_op jit(solution)/shard_map/ppermute | solution.py:21
  81.3 3.0 constant_dynamic-slice_fusion.1.refs_0_
  84.3 5.1 %collective-permute-done.12.refs_5_ = bf16[512,384]{1,0:T(8,128)(2,1)S(1)} collective-permute-done((bf16[512,384]{1,0:T(8,128)(2,1)S(1)}, bf16[512,384]{1,0:T(8,128)(2,1)S(1)}, u32[]{:S(2)}, u32[]{:S(2)}) %collective-permute-start.12) | collective-permute-done | bytes 393248 | tf_op jit(solution)/shard_map/ppermute | solution.py:21
  89.5 6.4 %collective-permute-done.13.refs_7_ = bf16[512,384]{1,0:T(8,128)(2,1)S(1)} collective-permute-done((bf16[512,384]{1,0:T(8,128)(2,1)S(1)}, bf16[512,384]{1,0:T(8,128)(2,1)S(1)}, u32[]{:S(2)}, u32[]{:S(2)}) %collective-permute-start.13) | collective-permute-done | bytes 393248 | tf_op jit(solution)/shard_map/ppermute | solution.py:21
  97.9 4.1 %shard_map.49 = (bf16[4,384,512]{2,1,0:T(8,128)(2,1)}, bf16[4,384,512]{2,1,0:T(8,128)(2,1)}, bf16[512,1536]{1,0:T(8,128)(2,1)}) custom-call(bf16[512,384]{1,0:T(8,128)(2,1)S(1)} %copy-done.24, bf16[512,384]{1,0:T(8,128)(2,1)S(1)} %copy-done.26, bf16[512,384]{1,0:T(8,128)(2,1)S(1)} %copy-done.16, bf16[512,384]{1,0:T(8,128)(2,1)S(1)} %collective-permute-done.11.refs_3_, ...), custom_call_target="tpu_custom_call" | custom-call | tf_op jit(solution)/shard_map/pallas_call | solution.py:66
  102.0 11.1 %collective-permute-done.6.refs_2_ = bf16[768,384]{1,0:T(8,128)(2,1)} collective-permute-done((bf16[768,384]{1,0:T(8,128)(2,1)}, bf16[768,384]{1,0:T(8,128)(2,1)}, u32[]{:S(2)}, u32[]{:S(2)}) %collective-permute-start.6) | collective-permute-done | bytes 589856 | tf_op jit(solution)/shard_map/ppermute | solution.py:21
  113.1 3.9 %collective-permute-done.4.refs_1_ = bf16[768,384]{1,0:T(8,128)(2,1)} collective-permute-done((bf16[768,384]{1,0:T(8,128)(2,1)}, bf16[768,384]{1,0:T(8,128)(2,1)}, u32[]{:S(2)}, u32[]{:S(2)}) %collective-permute-start.4) | collective-permute-done | bytes 589856 | tf_op jit(solution)/shard_map/ppermute | solution.py:21
  118.4 4.2 %collective-permute-start.22 = (bf16[512,1536]{1,0:T(8,128)(2,1)S(1)}, bf16[512,1536]{1,0:T(8,128)(2,1)}, u32[]{:S(2)}, u32[]{:S(2)}) collective-permute-start(bf16[512,1536]{1,0:T(8,128)(2,1)S(1)} %copy-done.7), channel_id=1, source_target_pairs={{1,0},{0,1},{3,2},{2,3},{5,4},{4,5},{7,6},{6,7},{9,8},{8,9},{11,10... | collective-permute-start | bytes 4718600 | tf_op jit(solution)/shard_map/ppermute | solution.py:21
  126.8 13.8 %shard_map.50.refs_7_ = f32[768,1536]{1,0:T(8,128)} custom-call(s32[1]{0:T(128)} %bitcast.9.first_ref, bf16[768,384]{1,0:T(8,128)(2,1)S(1)} %bitcast.65, bf16[768,384]{1,0:T(8,128)(2,1)} %collective-permute-done.4.refs_1_, bf16[768,384]{1,0:T(8,128)(2,1)} %collective-permute-done.6.refs_2_, bf16[768,384]{1,0:T(8,128)(2,1)} %collective-permute-done.8.refs_3_, ...), custom_call_target="tpu_custom_call" | custom-call | tf_op jit(solution)/shard_map/pallas_call | solution.py:106
  140.6 9.9 %collective-permute-done.7.refs_2_ = bf16[768,384]{1,0:T(8,128)(2,1)} collective-permute-done((bf16[768,384]{1,0:T(8,128)(2,1)}, bf16[768,384]{1,0:T(8,128)(2,1)}, u32[]{:S(2)}, u32[]{:S(2)}) %collective-permute-start.7) | collective-permute-done | bytes 589856 | tf_op jit(solution)/shard_map/ppermute | solution.py:21
  150.5 12.6 %collective-permute-done.5.refs_1_ = bf16[768,384]{1,0:T(8,128)(2,1)} collective-permute-done((bf16[768,384]{1,0:T(8,128)(2,1)}, bf16[768,384]{1,0:T(8,128)(2,1)}, u32[]{:S(2)}, u32[]{:S(2)}) %collective-permute-start.5) | collective-permute-done | bytes 589856 | tf_op jit(solution)/shard_map/ppermute | solution.py:21
  163.1 12.8 %shard_map.51 = bf16[768,1536]{1,0:T(8,128)(2,1)} custom-call(s32[1]{0:T(128)} %bitcast.9.first_ref, bf16[768,384]{1,0:T(8,128)(2,1)S(1)} %copy-done.9, bf16[768,384]{1,0:T(8,128)(2,1)} %collective-permute-done.5.refs_1_, bf16[768,384]{1,0:T(8,128)(2,1)} %collective-permute-done.7.refs_2_, bf16[768,384]{1,0:T(8,128)(2,1)} %collective-permute-done.9.refs_3_, ...), custom_call_target="tpu_custom_call" | custom-call | tf_op jit(solution)/shard_map/pallas_call | solution.py:106
  175.9 2.4 dynamic-slice_bitcast_fusion.1
  183.4 13.8 %shard_map.53.refs_7_ = f32[768,1536]{1,0:T(8,128)} custom-call(s32[1]{0:T(128)} %bitcast.9.first_ref, bf16[768,384]{1,0:T(8,128)(2,1)S(1)} %bitcast.66, bf16[768,384]{1,0:T(8,128)(2,1)} %collective-permute-done.4.refs_1_, bf16[768,384]{1,0:T(8,128)(2,1)} %collective-permute-done.6.refs_2_, bf16[768,384]{1,0:T(8,128)(2,1)} %collective-permute-done.8.refs_3_, ...), custom_call_target="tpu_custom_call" | custom-call | tf_op jit(solution)/shard_map/pallas_call | solution.py:106
  197.2 2.6 fusion.1.refs_1_
  202.2 12.8 %shard_map.54 = bf16[768,1536]{1,0:T(8,128)(2,1)} custom-call(s32[1]{0:T(128)} %bitcast.9.first_ref, bf16[768,384]{1,0:T(8,128)(2,1)S(1)} %copy-done.10, bf16[768,384]{1,0:T(8,128)(2,1)} %collective-permute-done.5.refs_1_, bf16[768,384]{1,0:T(8,128)(2,1)} %collective-permute-done.7.refs_2_, bf16[768,384]{1,0:T(8,128)(2,1)} %collective-permute-done.9.refs_3_, ...), custom_call_target="tpu_custom_call" | custom-call | tf_op jit(solution)/shard_map/pallas_call | solution.py:106
  219.4 2.6 fusion
  223.0 21.1 %collective-permute-done.24 = bf16[2,192,1536]{2,1,0:T(8,128)(2,1)} collective-permute-done((bf16[2,192,1536]{2,1,0:T(8,128)(2,1)S(1)}, bf16[2,192,1536]{2,1,0:T(8,128)(2,1)}, u32[]{:S(2)}, u32[]{:S(2)}) %collective-permute-start.24) | collective-permute-done | bytes 1179680 | tf_op jit(solution)/shard_map/ppermute | solution.py:21
  246.0 23.5 %collective-permute-done.26 = bf16[2,192,1536]{2,1,0:T(8,128)(2,1)} collective-permute-done((bf16[2,192,1536]{2,1,0:T(8,128)(2,1)}, bf16[2,192,1536]{2,1,0:T(8,128)(2,1)}, u32[]{:S(2)}, u32[]{:S(2)}) %collective-permute-start.26) | collective-permute-done | bytes 1179680 | tf_op jit(solution)/shard_map/ppermute | solution.py:21
  273.0 13.2 %shard_map.57 = bf16[384,2560]{1,0:T(8,128)(2,1)} custom-call(s32[9]{0:T(128)S(1)} %concatenate.20.scalar_ref, bf16[2,384,1536]{2,1,0:T(8,128)(2,1)S(1)} %bitcast.56, bf16[2,384,1536]{2,1,0:T(8,128)(2,1)} %bitcast.60, bf16[8,2560,384]{2,1,0:T(8,128)(2,1)} %bitcast.67, bf16[8,2560,384]{2,1,0:T(8,128)(2,1)} %bitcast.68), custom_call_target="tpu_custom_call" | custom-call | tf_op jit(solution)/shard_map/pallas_call | solution.py:159
  289.2 13.5 %shard_map.56.refs_1_ = f32[384,2560]{1,0:T(8,128)} custom-call(s32[9]{0:T(128)S(1)} %concatenate.18.scalar_ref, bf16[2,384,1536]{2,1,0:T(8,128)(2,1)S(1)} %bitcast.57, bf16[2,384,1536]{2,1,0:T(8,128)(2,1)S(1)} %bitcast.61, bf16[8,2560,384]{2,1,0:T(8,128)(2,1)} %bitcast.69, bf16[8,2560,384]{2,1,0:T(8,128)(2,1)} %bitcast.70), custom_call_target="tpu_custom_call" | custom-call | tf_op jit(solution)/shard_map/pallas_call | solution.py:159
  304.3 5.0 %shard_map.61 = bf16[384,512]{1,0:T(8,128)(2,1)S(1)} custom-call(s32[9]{0:T(128)S(1)} %concatenate.20.scalar_ref, bf16[2,384,1536]{2,1,0:T(8,128)(2,1)S(1)} %bitcast.58, bf16[2,384,1536]{2,1,0:T(8,128)(2,1)S(1)} %bitcast.62, bf16[8,512,384]{2,1,0:T(8,128)(2,1)} %shard_map.59.refs_2_.refs_3_, bf16[8,512,384]{2,1,0:T(8,128)(2,1)} %shard_map.59.refs_2_.refs_3_), custom_call_target="tpu_custom_call" | custom-call | tf_op jit(solution)/shard_map/pallas_call | solution.py:159
  309.7 5.2 %shard_map.60 = f32[384,512]{1,0:T(8,128)S(1)} custom-call(s32[9]{0:T(128)S(1)} %concatenate.18.scalar_ref, bf16[2,384,1536]{2,1,0:T(8,128)(2,1)S(1)} %bitcast.59, bf16[2,384,1536]{2,1,0:T(8,128)(2,1)S(1)} %bitcast.63, bf16[8,512,384]{2,1,0:T(8,128)(2,1)} %shard_map.59.refs_2_.refs_3_, bf16[8,512,384]{2,1,0:T(8,128)(2,1)} %shard_map.59.refs_2_.refs_3_), custom_call_target="tpu_custom_call" | custom-call | tf_op jit(solution)/shard_map/pallas_call | solution.py:159
  315.0 22.9 %collective-permute-done.28 = bf16[384,512]{1,0:T(8,128)(2,1)S(1)} collective-permute-done((bf16[384,512]{1,0:T(8,128)(2,1)S(1)}, bf16[384,512]{1,0:T(8,128)(2,1)S(1)}, u32[]{:S(2)}, u32[]{:S(2)}) %collective-permute-start.28) | collective-permute-done | bytes 393248 | tf_op jit(solution)/shard_map/ppermute | solution.py:21
  (148 shorter events, 57.9 us)
Async XLA Ops:
  6.5 266.5 %all-gather.5.cloned.1.call-start = ((), (), s32[]{:S(2)}) async-start(), calls=%async_computation | async-start | bytes 17694720 | tf_op jit(solution)/shard_map/all_gather | solution.py:216
  15.0 36.5 %collective-permute-start.1 = (bf16[512,384]{1,0:T(8,128)(2,1)S(1)}, bf16[512,384]{1,0:T(8,128)(2,1)S(1)}, u32[]{:S(2)}, u32[]{:S(2)}) collective-permute-start(bf16[512,384]{1,0:T(8,128)(2,1)S(1)} %pad_maximum_fusion.3.refs_0_), channel_id=1, source_target_pairs={{8,0},{12,4},{0,8},{4,12},{9,1},{13,5},{1,9},{5,13},{10,2},{14,6},... | collective-permute-start | bytes 1179656 | tf_op jit(solution)/shard_map/ppermute | solution.py:21
  17.4 33.2 %collective-permute-start.2 = (bf16[512,384]{1,0:T(8,128)(2,1)S(1)}, bf16[512,384]{1,0:T(8,128)(2,1)S(1)}, u32[]{:S(2)}, u32[]{:S(2)}) collective-permute-start(bf16[512,384]{1,0:T(8,128)(2,1)S(1)} %pad_maximum_fusion.3.refs_0_), channel_id=1, source_target_pairs={{4,0},{8,4},{12,8},{0,12},{5,1},{9,5},{13,9},{1,13},{6,2},{10,6},{... | collective-permute-start | bytes 1179656 | tf_op jit(solution)/shard_map/ppermute | solution.py:21
  20.5 37.9 %collective-permute-start = (bf16[768,384]{1,0:T(8,128)(2,1)S(1)}, bf16[768,384]{1,0:T(8,128)(2,1)S(1)}, u32[]{:S(2)}, u32[]{:S(2)}) collective-permute-start(bf16[768,384]{1,0:T(8,128)(2,1)S(1)} %bitcast.64), channel_id=1, source_target_pairs={{2,0},{0,2},{3,1},{1,3},{6,4},{4,6},{7,5},{5,7},{10,8},{8,10},{11,... | collective-permute-start | bytes 1769480 | tf_op jit(solution)/shard_map/ppermute | solution.py:21
  22.6 29.6 %collective-permute-start.3 = (bf16[512,384]{1,0:T(8,128)(2,1)S(1)}, bf16[512,384]{1,0:T(8,128)(2,1)S(1)}, u32[]{:S(2)}, u32[]{:S(2)}) collective-permute-start(bf16[512,384]{1,0:T(8,128)(2,1)S(1)} %pad_maximum_fusion.3.refs_0_), channel_id=1, source_target_pairs={{12,0},{0,4},{4,8},{8,12},{13,1},{1,5},{5,9},{9,13},{14,2},{2,6},{... | collective-permute-start | bytes 1179656 | tf_op jit(solution)/shard_map/ppermute | solution.py:21
  23.9 32.6 %collective-permute-start.10 = (bf16[512,384]{1,0:T(8,128)(2,1)S(1)}, bf16[512,384]{1,0:T(8,128)(2,1)S(1)}, u32[]{:S(2)}, u32[]{:S(2)}) collective-permute-start(bf16[512,384]{1,0:T(8,128)(2,1)S(1)} %pad_maximum_fusion.3.refs_0_), channel_id=1, source_target_pairs={{16,0},{0,16},{17,1},{1,17},{18,2},{2,18},{19,3},{3,19},{20,4},{4,... | collective-permute-start | bytes 1179656 | tf_op jit(solution)/shard_map/ppermute | solution.py:21
  50.6 5.2 %collective-permute-start.14 = (bf16[256,384]{1,0:T(8,128)(2,1)S(1)}, bf16[256,384]{1,0:T(8,128)(2,1)S(1)}, u32[]{:S(2)}, u32[]{:S(2)}) collective-permute-start(bf16[256,384]{1,0:T(8,128)(2,1)S(1)} %copy-done.36), channel_id=1, source_target_pairs={{2,0},{0,2},{3,1},{1,3},{6,4},{4,6},{7,5},{5,7},{10,8},{8,10},{11,... | collective-permute-start | bytes 589832 | tf_op jit(solution)/shard_map/ppermute | solution.py:21
  51.6 8.4 %collective-permute-start.16 = (bf16[256,384]{1,0:T(8,128)(2,1)S(1)}, bf16[256,384]{1,0:T(8,128)(2,1)S(1)}, u32[]{:S(2)}, u32[]{:S(2)}) collective-permute-start(bf16[256,384]{1,0:T(8,128)(2,1)S(1)} %slice.12), channel_id=1, source_target_pairs={{2,0},{0,2},{3,1},{1,3},{6,4},{4,6},{7,5},{5,7},{10,8},{8,10},{11,... | collective-permute-start | bytes 589832 | tf_op jit(solution)/shard_map/ppermute | solution.py:21
  52.2 12.1 %collective-permute-start.18 = (bf16[256,384]{1,0:T(8,128)(2,1)S(1)}, bf16[256,384]{1,0:T(8,128)(2,1)}, u32[]{:S(2)}, u32[]{:S(2)}) collective-permute-start(bf16[256,384]{1,0:T(8,128)(2,1)S(1)} %slice.13), channel_id=1, source_target_pairs={{2,0},{0,2},{3,1},{1,3},{6,4},{4,6},{7,5},{5,7},{10,8},{8,10},{11,... | collective-permute-start | bytes 589832 | tf_op jit(solution)/shard_map/ppermute | solution.py:21
  55.7 12.7 %collective-permute-start.20 = (bf16[256,384]{1,0:T(8,128)(2,1)S(1)}, bf16[256,384]{1,0:T(8,128)(2,1)}, u32[]{:S(2)}, u32[]{:S(2)}) collective-permute-start(bf16[256,384]{1,0:T(8,128)(2,1)S(1)} %slice.14), channel_id=1, source_target_pairs={{2,0},{0,2},{3,1},{1,3},{6,4},{4,6},{7,5},{5,7},{10,8},{8,10},{11,... | collective-permute-start | bytes 589832 | tf_op jit(solution)/shard_map/ppermute | solution.py:21
  57.2 23.9 %collective-permute-start.11 = (bf16[512,384]{1,0:T(8,128)(2,1)S(1)}, bf16[512,384]{1,0:T(8,128)(2,1)S(1)}, u32[]{:S(2)}, u32[]{:S(2)}) collective-permute-start(bf16[512,384]{1,0:T(8,128)(2,1)S(1)} %collective-permute-done.2.refs_2_), channel_id=1, source_target_pairs={{16,0},{0,16},{17,1},{1,17},{18,2},{2,18},{19,3},{3,19},{20,4},{4,... | collective-permute-start | bytes 1179656 | tf_op jit(solution)/shard_map/ppermute | solution.py:21
  58.4 10.9 %collective-permute-start.15 = (bf16[256,384]{1,0:T(8,128)(2,1)S(1)}, bf16[256,384]{1,0:T(8,128)(2,1)S(1)}, u32[]{:S(2)}, u32[]{:S(2)}) collective-permute-start(bf16[256,384]{1,0:T(8,128)(2,1)S(1)} %collective-permute-done.14.refs_8_), channel_id=1, source_target_pairs={{16,0},{0,16},{17,1},{1,17},{18,2},{2,18},{19,3},{3,19},{20,4},{4,... | collective-permute-start | bytes 589832 | tf_op jit(solution)/shard_map/ppermute | solution.py:21
  59.9 11.5 %collective-permute-start.17 = (bf16[256,384]{1,0:T(8,128)(2,1)S(1)}, bf16[256,384]{1,0:T(8,128)(2,1)S(1)}, u32[]{:S(2)}, u32[]{:S(2)}) collective-permute-start(bf16[256,384]{1,0:T(8,128)(2,1)S(1)} %collective-permute-done.16.refs_10_), channel_id=1, source_target_pairs={{16,0},{0,16},{17,1},{1,17},{18,2},{2,18},{19,3},{3,19},{20,4},{4,... | collective-permute-start | bytes 589832 | tf_op jit(solution)/shard_map/ppermute | solution.py:21
  64.3 11.4 %collective-permute-start.19 = (bf16[256,384]{1,0:T(8,128)(2,1)}, bf16[256,384]{1,0:T(8,128)(2,1)S(1)}, u32[]{:S(2)}, u32[]{:S(2)}) collective-permute-start(bf16[256,384]{1,0:T(8,128)(2,1)} %collective-permute-done.18.refs_12_), channel_id=1, source_target_pairs={{16,0},{0,16},{17,1},{1,17},{18,2},{2,18},{19,3},{3,19},{20,4},{4,... | collective-permute-start | bytes 589832 | tf_op jit(solution)/shard_map/ppermute | solution.py:21
  68.5 11.4 %collective-permute-start.21 = (bf16[256,384]{1,0:T(8,128)(2,1)}, bf16[256,384]{1,0:T(8,128)(2,1)}, u32[]{:S(2)}, u32[]{:S(2)}) collective-permute-start(bf16[256,384]{1,0:T(8,128)(2,1)} %collective-permute-done.20.refs_14_), channel_id=1, source_target_pairs={{16,0},{0,16},{17,1},{1,17},{18,2},{2,18},{19,3},{3,19},{20,4},{4,... | collective-permute-start | bytes 589832 | tf_op jit(solution)/shard_map/ppermute | solution.py:21
  69.3 32.7 %collective-permute-start.8 = (bf16[768,384]{1,0:T(8,128)(2,1)}, bf16[768,384]{1,0:T(8,128)(2,1)}, u32[]{:S(2)}, u32[]{:S(2)}) collective-permute-start(bf16[768,384]{1,0:T(8,128)(2,1)} %shard_map.48), channel_id=1, source_target_pairs={{12,0},{0,4},{4,8},{8,12},{13,1},{1,5},{5,9},{9,13},{14,2},{2,6},{... | collective-permute-start | bytes 1769480 | tf_op jit(solution)/shard_map/ppermute | solution.py:21
  72.1 41.0 %collective-permute-start.6 = (bf16[768,384]{1,0:T(8,128)(2,1)}, bf16[768,384]{1,0:T(8,128)(2,1)}, u32[]{:S(2)}, u32[]{:S(2)}) collective-permute-start(bf16[768,384]{1,0:T(8,128)(2,1)} %shard_map.47), channel_id=1, source_target_pairs={{8,0},{12,4},{0,8},{4,12},{9,1},{13,5},{1,9},{5,13},{10,2},{14,6},... | collective-permute-start | bytes 1769480 | tf_op jit(solution)/shard_map/ppermute | solution.py:21
  76.3 40.6 %collective-permute-start.4 = (bf16[768,384]{1,0:T(8,128)(2,1)}, bf16[768,384]{1,0:T(8,128)(2,1)}, u32[]{:S(2)}, u32[]{:S(2)}) collective-permute-start(bf16[768,384]{1,0:T(8,128)(2,1)} %shard_map.46), channel_id=1, source_target_pairs={{4,0},{8,4},{12,8},{0,12},{5,1},{9,5},{13,9},{1,13},{6,2},{10,6},{... | collective-permute-start | bytes 1769480 | tf_op jit(solution)/shard_map/ppermute | solution.py:21
  79.9 9.6 %collective-permute-start.12 = (bf16[512,384]{1,0:T(8,128)(2,1)S(1)}, bf16[512,384]{1,0:T(8,128)(2,1)S(1)}, u32[]{:S(2)}, u32[]{:S(2)}) collective-permute-start(bf16[512,384]{1,0:T(8,128)(2,1)S(1)} %copy-done.14), channel_id=1, source_target_pairs={{16,0},{0,16},{17,1},{1,17},{18,2},{2,18},{19,3},{3,19},{20,4},{4,... | collective-permute-start | bytes 1179656 | tf_op jit(solution)/shard_map/ppermute | solution.py:21
  81.1 14.7 %collective-permute-start.13 = (bf16[512,384]{1,0:T(8,128)(2,1)S(1)}, bf16[512,384]{1,0:T(8,128)(2,1)S(1)}, u32[]{:S(2)}, u32[]{:S(2)}) collective-permute-start(bf16[512,384]{1,0:T(8,128)(2,1)S(1)} %copy-done.18), channel_id=1, source_target_pairs={{16,0},{0,16},{17,1},{1,17},{18,2},{2,18},{19,3},{3,19},{20,4},{4,... | collective-permute-start | bytes 1179656 | tf_op jit(solution)/shard_map/ppermute | solution.py:21
  117.0 185.7 %all-gather.7.cloned.1.call-start = ((), (), s32[]{:S(2)}) async-start(), calls=%async_computation.1 | async-start | bytes 3538944 | tf_op jit(solution)/shard_map/all_gather | solution.py:216
  118.4 7.3 %collective-permute-start.22 = (bf16[512,1536]{1,0:T(8,128)(2,1)S(1)}, bf16[512,1536]{1,0:T(8,128)(2,1)}, u32[]{:S(2)}, u32[]{:S(2)}) collective-permute-start(bf16[512,1536]{1,0:T(8,128)(2,1)S(1)} %copy-done.7), channel_id=1, source_target_pairs={{1,0},{0,1},{3,2},{2,3},{5,4},{4,5},{7,6},{6,7},{9,8},{8,9},{11,10... | collective-permute-start | bytes 4718600 | tf_op jit(solution)/shard_map/ppermute | solution.py:21
  122.5 18.0 %collective-permute-start.9 = (bf16[768,384]{1,0:T(8,128)(2,1)}, bf16[768,384]{1,0:T(8,128)(2,1)}, u32[]{:S(2)}, u32[]{:S(2)}) collective-permute-start(bf16[768,384]{1,0:T(8,128)(2,1)} %collective-permute-done.8.refs_3_), channel_id=1, source_target_pairs={{2,0},{0,2},{3,1},{1,3},{6,4},{4,6},{7,5},{5,7},{10,8},{8,10},{11,... | collective-permute-start | bytes 1769480 | tf_op jit(solution)/shard_map/ppermute | solution.py:21
  123.8 26.7 %collective-permute-start.7 = (bf16[768,384]{1,0:T(8,128)(2,1)}, bf16[768,384]{1,0:T(8,128)(2,1)}, u32[]{:S(2)}, u32[]{:S(2)}) collective-permute-start(bf16[768,384]{1,0:T(8,128)(2,1)} %collective-permute-done.6.refs_2_), channel_id=1, source_target_pairs={{2,0},{0,2},{3,1},{1,3},{6,4},{4,6},{7,5},{5,7},{10,8},{8,10},{11,... | collective-permute-start | bytes 1769480 | tf_op jit(solution)/shard_map/ppermute | solution.py:21
  124.0 39.1 %collective-permute-start.5 = (bf16[768,384]{1,0:T(8,128)(2,1)}, bf16[768,384]{1,0:T(8,128)(2,1)}, u32[]{:S(2)}, u32[]{:S(2)}) collective-permute-start(bf16[768,384]{1,0:T(8,128)(2,1)} %collective-permute-done.4.refs_1_), channel_id=1, source_target_pairs={{2,0},{0,2},{3,1},{1,3},{6,4},{4,6},{7,5},{5,7},{10,8},{8,10},{11,... | collective-permute-start | bytes 1769480 | tf_op jit(solution)/shard_map/ppermute | solution.py:21
  126.8 36.3 %copy-start.11 = (bf16[4,384,512]{2,1,0:T(8,128)(2,1)S(1)}, bf16[4,384,512]{2,1,0:T(8,128)(2,1)}, u32[]{:S(2)}) copy-start(bf16[4,384,512]{2,1,0:T(8,128)(2,1)} %get-tuple-element.8.refs_4_.refs_0_) | copy-start | bytes 4718596
  178.3 18.8 %collective-permute-start.23 = (bf16[2,192,1536]{2,1,0:T(8,128)(2,1)}, bf16[2,192,1536]{2,1,0:T(8,128)(2,1)}, u32[]{:S(2)}, u32[]{:S(2)}) collective-permute-start(bf16[2,192,1536]{2,1,0:T(8,128)(2,1)} %dynamic-slice_bitcast_fusion.1), channel_id=1, source_target_pairs={{1,0},{0,1},{3,2},{2,3},{5,4},{4,5},{7,6},{6,7},{9,8},{8,9},{11,10... | collective-permute-start | bytes 3538952 | tf_op jit(solution)/shard_map/ppermute | solution.py:21
  216.5 2.9 collective-permute-start.25
  216.8 27.4 %collective-permute-start.24 = (bf16[2,192,1536]{2,1,0:T(8,128)(2,1)S(1)}, bf16[2,192,1536]{2,1,0:T(8,128)(2,1)}, u32[]{:S(2)}, u32[]{:S(2)}) collective-permute-start(bf16[2,192,1536]{2,1,0:T(8,128)(2,1)S(1)} %copy-done.32), channel_id=1, source_target_pairs={{16,0},{0,16},{17,1},{1,17},{18,2},{2,18},{19,3},{3,19},{20,4},{4,... | collective-permute-start | bytes 3538952 | tf_op jit(solution)/shard_map/ppermute | solution.py:21
  222.0 47.4 %collective-permute-start.26 = (bf16[2,192,1536]{2,1,0:T(8,128)(2,1)}, bf16[2,192,1536]{2,1,0:T(8,128)(2,1)}, u32[]{:S(2)}, u32[]{:S(2)}) collective-permute-start(bf16[2,192,1536]{2,1,0:T(8,128)(2,1)} %fusion), channel_id=1, source_target_pairs={{16,0},{0,16},{17,1},{1,17},{18,2},{2,18},{19,3},{3,19},{20,4},{4,... | collective-permute-start | bytes 3538952 | tf_op jit(solution)/shard_map/ppermute | solution.py:21
  286.2 51.9 %collective-permute-start.27 = (bf16[384,2560]{1,0:T(8,128)(2,1)}, bf16[384,2560]{1,0:T(8,128)(2,1)}, u32[]{:S(2)}, u32[]{:S(2)}) collective-permute-start(bf16[384,2560]{1,0:T(8,128)(2,1)} %shard_map.57), channel_id=1, source_target_pairs={{2,0},{0,2},{3,1},{1,3},{6,4},{4,6},{7,5},{5,7},{10,8},{8,10},{11,... | collective-permute-start | bytes 5898248 | tf_op jit(solution)/shard_map/ppermute | solution.py:21
  309.3 28.6 %collective-permute-start.28 = (bf16[384,512]{1,0:T(8,128)(2,1)S(1)}, bf16[384,512]{1,0:T(8,128)(2,1)S(1)}, u32[]{:S(2)}, u32[]{:S(2)}) collective-permute-start(bf16[384,512]{1,0:T(8,128)(2,1)S(1)} %shard_map.61), channel_id=1, source_target_pairs={{2,0},{0,2},{3,1},{1,3},{6,4},{4,6},{7,5},{5,7},{10,8},{8,10},{11,... | collective-permute-start | bytes 1179656 | tf_op jit(solution)/shard_map/ppermute | solution.py:21
  (37 other events, 347.3 us)
Sparse Core Ops, SparseCore 0:
  117.1 144.4 all-gather.4
  263.3 38.5 all-gather.6

commit v3 on v2

--- a/solution.py
+++ b/solution.py
@@ -7,7 +7,7 @@
 
 damping = 0.1
 pair = 2
-shares = (5, 1)
+shares = (3, 1)
 f32 = jnp.float32
 bf16 = jnp.bfloat16
 params = pltpu.CompilerParams(vmem_limit_bytes=48 * 2**20)
@@ -41,11 +41,6 @@
 
 def square(v):
     return (v.astype(f32) ** 2).astype(bf16)
-
-
-def tile(size, most):
-    fits = [t for t in range(128, most + 1, 128) if size % t == 0]
-    return max(fits) if fits else size
 
 
 def pack(groups, others, rows):
@@ -70,19 +65,17 @@
     )(*[v for group in groups + others for v in group])
 
 
-def mix(rows, left, rights, first, part, parts, kind, carry=None):
+def mix(rows, left, rights, first, start, runs, kind, carry=None):
     count, cols, tok = left.shape
     n = rows[0].shape[0]
-    span = rights[0].shape[1] // parts
-    tj = tile(span, 768)
-    runs = span // tj
+    tj = rights[0].shape[1] // 2
     group = 2 if count % 2 == 0 and cols % 128 == 0 else 1
 
     def body(first_ref, *refs):
         row_refs, left_ref, refs = refs[:count], refs[count], refs[count + 1 :]
         right_refs, out_ref = refs[: len(rights)], refs[-1]
         j = pl.program_id(0)
-        b = jnp.where(j // runs == first_ref[0], right_refs[0][...], right_refs[1][...])
+        b = jnp.where(j % 2 == first_ref[0], right_refs[0][...], right_refs[1][...])
         b2 = square(b)
         total = refs[len(rights)][...] if carry is not None else None
         for k in range(0, count, group):
@@ -98,17 +91,17 @@
 
     specs = [pl.BlockSpec((n, cols), lambda j, f: (0, 0)) for _ in rows]
     specs += [pl.BlockSpec((count, cols, tok), lambda j, f: (0, 0, 0))]
-    specs += [pl.BlockSpec((tok, tj), lambda j, f: (0, part * runs + j % runs)) for _ in rights]
+    specs += [pl.BlockSpec((tok, tj), lambda j, f: (0, start + j // 2)) for _ in rights]
     args = [*rows, left, *rights]
     if carry is not None:
-        specs.append(pl.BlockSpec((n, tj), lambda j, f: (0, j)))
+        specs.append(pl.BlockSpec((n, tj), lambda j, f: (0, 2 * start + j)))
         args.append(carry)
     return pl.pallas_call(
         body,
-        out_shape=jax.ShapeDtypeStruct((n, span * len(rights)), kind),
+        out_shape=jax.ShapeDtypeStruct((n, 2 * runs * tj), kind),
         grid_spec=pltpu.PrefetchScalarGridSpec(
             num_scalar_prefetch=1,
-            grid=(runs * len(rights),),
+            grid=(2 * runs,),
             in_specs=specs,
             out_specs=pl.BlockSpec((n, tj), lambda j, f: (0, j)),
         ),
@@ -215,16 +208,15 @@
         raw = after(raw, *gate) if gate else raw
         wides.append(lax.all_gather(raw, ("z", "c"), axis=0))
 
-    parts = [mix(in_own, left, rights, at["c"], h, 2, f32) for h in range(2)]
+    own = mix(in_own, left, rights, at["c"], 0, 2, f32)
     halves = []
     take = lambda v, axis, i: lax.dynamic_index_in_dim(v, i, axis, keepdims=False)
     for h in range(2):
-        ready = after(left_other, mine) if h else left_other
-        part = mix(in_other, ready, rights, at["c"], h, 2, bf16, parts[h])
+        part = mix(in_other, left_other, rights, at["c"], h, 1, bf16, own)
         view = part.reshape(pair, pair, share, -1)
         away = fetch(take(view, 1, 1 - at["c"]), "c")
         mine = (take(view, 1, at["c"]).astype(f32) + away.astype(f32)).astype(bf16)
-        got = gather(mine, "y")
+        got = gather(after(mine, *got[1:]) if h else mine, "y")
         full = jnp.stack(
             [lax.select_n((ny + j - at["y"]) % ny, *got) if ny > 2 else
              jnp.where(at["y"] == j, got[0], got[-1]) for j in range(ny)], axis=1)

time: 352 us -> 339 us (0.963)
  waiting for transfers between devices: 164 us -> 155 us
    ppermute x29, waiting for transfers between devices: 164 us -> 139 us  [fetch(): return lax.ppermute(value, axis, pairs(lax.axis_size(axis), shift))]
    all_gather x2, waiting for transfers between devices: 0.01 us -> 16.4 us  [shards(): wides.append(lax.all_gather(raw, ('z', 'c'), axis=0))]
    pallas_call x4 -> x3, Pallas kernels: 53.2 us -> 50.6 us  [mix(): pl.pallas_call(body, out_shape=jax.ShapeDtypeStruct((n, 2 * runs * tj), k...]
  transfers between devices with their start and end apart: 31 -> 31, of which waited for: 19 -> 18; matrix products, arithmetic and copies ran while one was open for 6% -> 6% of each run, Pallas kernels for 27% -> 27%
where the time goes in v3:
time: 339 us; the launch traced here: 335 us
  waiting for transfers between devices  155 us (46%)
  Pallas kernels  91.8 us (27%)
  local copies, waits for them, and re-layouts  30.8 us (9%)
  starting transfers between devices  26.7 us (8%)
  between operations  13.8 us (4%)
  other arithmetic  10.2 us (3%)
  matrix products  6.08 us (2%)
    ppermute x29, waiting for transfers between devices, fetch(): return lax.ppermute(value, axis, pairs(lax.axis_size(axis), shift))  139 us
    pallas_call x3, Pallas kernels, mix(): pl.pallas_call(body, out_shape=jax.ShapeDtypeStruct((n, 2 * runs * tj), k...  50.6 us
    pallas_call x4, Pallas kernels, expand(): pl.pallas_call(body, out_shape=jax.ShapeDtypeStruct((n, wide), kind), gri...  37.1 us
    ppermute x29, starting transfers between devices, fetch(): return lax.ppermute(value, axis, pairs(lax.axis_size(axis), shift))  26.5 us
    unnamed x76, local copies, waits for them, and re-layouts  17.1 us
    all_gather x2, waiting for transfers between devices, shards(): wides.append(lax.all_gather(raw, ('z', 'c'), axis=0))  16.4 us
  transfers between devices with their start and end apart: 31, of which 18 were waited for; matrix products, arithmetic and copies ran while one was open for 6% of the time, Pallas kernels for 27%

profile of v3, /device:TPU:9, one launch (start us, length us, event | category | flops | bytes accessed | tf_op | source)
XLA Modules:
  0.0 334.8 jit_solution(15057573589100156741)
XLA Ops:
  8.4 4.3 %convolution_convert_fusion.1 = bf16[256,384]{1,0:T(8,128)(2,1)S(1)} fusion(bf16[256,6144]{1,0:T(8,128)(2,1)S(1)} %copy-done, bf16[6144,384]{1,0:T(8,128)(2,1)} %param.6), kind=kOutput, calls=%fused_computation.16 | convolution fusion | flops 1208057856 | bytes 8060928 | tf_op jit(solution)/shard_map/dot_general | solution.py:174
  15.0 2.4 collective-permute-start.1
  17.6 2.9 constant_dynamic-slice_fusion.2
  25.0 25.5 %collective-permute-done.2.refs_2_ = bf16[512,384]{1,0:T(8,128)(2,1)S(1)} collective-permute-done((bf16[512,384]{1,0:T(8,128)(2,1)S(1)}, bf16[512,384]{1,0:T(8,128)(2,1)S(1)}, u32[]{:S(2)}, u32[]{:S(2)}) %collective-permute-start.2) | collective-permute-done | bytes 393248 | tf_op jit(solution)/shard_map/ppermute | solution.py:21
  53.2 2.5 collective-permute-done.14.refs_8_
  60.6 3.6 %collective-permute-done.18.refs_12_ = bf16[256,384]{1,0:T(8,128)(2,1)} collective-permute-done((bf16[256,384]{1,0:T(8,128)(2,1)S(1)}, bf16[256,384]{1,0:T(8,128)(2,1)}, u32[]{:S(2)}, u32[]{:S(2)}) %collective-permute-start.18) | collective-permute-done | bytes 196640 | tf_op jit(solution)/shard_map/ppermute | solution.py:21
  65.0 3.5 %collective-permute-done.20.refs_14_ = bf16[256,384]{1,0:T(8,128)(2,1)} collective-permute-done((bf16[256,384]{1,0:T(8,128)(2,1)S(1)}, bf16[256,384]{1,0:T(8,128)(2,1)}, u32[]{:S(2)}, u32[]{:S(2)}) %collective-permute-start.20) | collective-permute-done | bytes 196640 | tf_op jit(solution)/shard_map/ppermute | solution.py:21
  69.3 2.1 collective-permute-done.17.refs_11_
  72.1 3.5 %collective-permute-done.19.refs_13_ = bf16[256,384]{1,0:T(8,128)(2,1)S(1)} collective-permute-done((bf16[256,384]{1,0:T(8,128)(2,1)}, bf16[256,384]{1,0:T(8,128)(2,1)S(1)}, u32[]{:S(2)}, u32[]{:S(2)}) %collective-permute-start.19) | collective-permute-done | bytes 196640 | tf_op jit(solution)/shard_map/ppermute | solution.py:21
  76.3 3.5 %collective-permute-done.21.refs_15_ = bf16[256,384]{1,0:T(8,128)(2,1)} collective-permute-done((bf16[256,384]{1,0:T(8,128)(2,1)}, bf16[256,384]{1,0:T(8,128)(2,1)}, u32[]{:S(2)}, u32[]{:S(2)}) %collective-permute-start.21) | collective-permute-done | bytes 196640 | tf_op jit(solution)/shard_map/ppermute | solution.py:21
  81.3 2.9 constant_dynamic-slice_fusion.1.refs_0_
  84.2 5.2 %collective-permute-done.12.refs_5_ = bf16[512,384]{1,0:T(8,128)(2,1)S(1)} collective-permute-done((bf16[512,384]{1,0:T(8,128)(2,1)S(1)}, bf16[512,384]{1,0:T(8,128)(2,1)S(1)}, u32[]{:S(2)}, u32[]{:S(2)}) %collective-permute-start.12) | collective-permute-done | bytes 393248 | tf_op jit(solution)/shard_map/ppermute | solution.py:21
  89.5 6.4 %collective-permute-done.13.refs_7_ = bf16[512,384]{1,0:T(8,128)(2,1)S(1)} collective-permute-done((bf16[512,384]{1,0:T(8,128)(2,1)S(1)}, bf16[512,384]{1,0:T(8,128)(2,1)S(1)}, u32[]{:S(2)}, u32[]{:S(2)}) %collective-permute-start.13) | collective-permute-done | bytes 393248 | tf_op jit(solution)/shard_map/ppermute | solution.py:21
  97.9 4.1 %shard_map.49 = (bf16[4,384,512]{2,1,0:T(8,128)(2,1)}, bf16[4,384,512]{2,1,0:T(8,128)(2,1)}, bf16[512,1536]{1,0:T(8,128)(2,1)}) custom-call(bf16[512,384]{1,0:T(8,128)(2,1)S(1)} %copy-done.23, bf16[512,384]{1,0:T(8,128)(2,1)S(1)} %copy-done.25, bf16[512,384]{1,0:T(8,128)(2,1)S(1)} %copy-done.14, bf16[512,384]{1,0:T(8,128)(2,1)S(1)} %collective-permute-done.11.refs_3_, ...), custom_call_target="tpu_custom_call" | custom-call | tf_op jit(solution)/shard_map/pallas_call | solution.py:61
  102.0 11.1 %collective-permute-done.6.refs_2_ = bf16[768,384]{1,0:T(8,128)(2,1)} collective-permute-done((bf16[768,384]{1,0:T(8,128)(2,1)}, bf16[768,384]{1,0:T(8,128)(2,1)}, u32[]{:S(2)}, u32[]{:S(2)}) %collective-permute-start.6) | collective-permute-done | bytes 589856 | tf_op jit(solution)/shard_map/ppermute | solution.py:21
  113.0 3.9 %collective-permute-done.4.refs_1_ = bf16[768,384]{1,0:T(8,128)(2,1)} collective-permute-done((bf16[768,384]{1,0:T(8,128)(2,1)}, bf16[768,384]{1,0:T(8,128)(2,1)}, u32[]{:S(2)}, u32[]{:S(2)}) %collective-permute-start.4) | collective-permute-done | bytes 589856 | tf_op jit(solution)/shard_map/ppermute | solution.py:21
  117.2 2.0 constant_dynamic-slice_fusion.refs_0_
  120.6 4.2 %collective-permute-start.22 = (bf16[512,1536]{1,0:T(8,128)(2,1)S(1)}, bf16[512,1536]{1,0:T(8,128)(2,1)}, u32[]{:S(2)}, u32[]{:S(2)}) collective-permute-start(bf16[512,1536]{1,0:T(8,128)(2,1)S(1)} %copy-done.8), channel_id=1, source_target_pairs={{1,0},{0,1},{3,2},{2,3},{5,4},{4,5},{7,6},{6,7},{9,8},{8,9},{11,10... | collective-permute-start | bytes 4718600 | tf_op jit(solution)/shard_map/ppermute | solution.py:21
  130.6 24.8 %shard_map.50.refs_7_ = f32[768,3072]{1,0:T(8,128)} custom-call(s32[1]{0:T(128)} %bitcast.9.first_ref, bf16[768,384]{1,0:T(8,128)(2,1)S(1)} %bitcast.65, bf16[768,384]{1,0:T(8,128)(2,1)} %collective-permute-done.4.refs_1_, bf16[768,384]{1,0:T(8,128)(2,1)} %collective-permute-done.6.refs_2_, bf16[768,384]{1,0:T(8,128)(2,1)} %collective-permute-done.8.refs_3_, ...), custom_call_target="tpu_custom_call" | custom-call | tf_op jit(solution)/shard_map/pallas_call | solution.py:99
  155.5 9.8 %collective-permute-done.5.refs_1_ = bf16[768,384]{1,0:T(8,128)(2,1)} collective-permute-done((bf16[768,384]{1,0:T(8,128)(2,1)}, bf16[768,384]{1,0:T(8,128)(2,1)}, u32[]{:S(2)}, u32[]{:S(2)}) %collective-permute-start.5) | collective-permute-done | bytes 589856 | tf_op jit(solution)/shard_map/ppermute | solution.py:21
  165.3 12.9 %shard_map.51 = bf16[768,1536]{1,0:T(8,128)(2,1)} custom-call(s32[1]{0:T(128)} %bitcast.9.first_ref, bf16[768,384]{1,0:T(8,128)(2,1)S(1)} %copy-done.6, bf16[768,384]{1,0:T(8,128)(2,1)} %collective-permute-done.5.refs_1_, bf16[768,384]{1,0:T(8,128)(2,1)} %collective-permute-done.7.refs_2_, bf16[768,384]{1,0:T(8,128)(2,1)} %collective-permute-done.9.refs_3_, ...), custom_call_target="tpu_custom_call" | custom-call | tf_op jit(solution)/shard_map/pallas_call | solution.py:99
  178.2 2.5 dynamic-slice_bitcast_fusion.1
  182.9 12.9 %shard_map.52 = bf16[768,1536]{1,0:T(8,128)(2,1)} custom-call(s32[1]{0:T(128)} %bitcast.9.first_ref, bf16[768,384]{1,0:T(8,128)(2,1)S(1)} %copy-done.6, bf16[768,384]{1,0:T(8,128)(2,1)} %collective-permute-done.5.refs_1_, bf16[768,384]{1,0:T(8,128)(2,1)} %collective-permute-done.7.refs_2_, bf16[768,384]{1,0:T(8,128)(2,1)} %collective-permute-done.9.refs_3_, ...), custom_call_target="tpu_custom_call" | custom-call | tf_op jit(solution)/shard_map/pallas_call | solution.py:99
  201.9 25.4 %collective-permute-done.24.refs_1_ = bf16[2,192,1536]{2,1,0:T(8,128)(2,1)} collective-permute-done((bf16[2,192,1536]{2,1,0:T(8,128)(2,1)S(1)}, bf16[2,192,1536]{2,1,0:T(8,128)(2,1)}, u32[]{:S(2)}, u32[]{:S(2)}) %collective-permute-start.24) | collective-permute-done | bytes 1179680 | tf_op jit(solution)/shard_map/ppermute | solution.py:21
  230.4 23.9 %collective-permute-done.26 = bf16[2,192,1536]{2,1,0:T(8,128)(2,1)} collective-permute-done((bf16[2,192,1536]{2,1,0:T(8,128)(2,1)}, bf16[2,192,1536]{2,1,0:T(8,128)(2,1)}, u32[]{:S(2)}, u32[]{:S(2)}) %collective-permute-start.26) | collective-permute-done | bytes 1179680 | tf_op jit(solution)/shard_map/ppermute | solution.py:21
  257.5 12.4 %shard_map.56 = bf16[384,2304]{1,0:T(8,128)(2,1)} custom-call(s32[9]{0:T(128)S(1)} %concatenate.20.scalar_ref, bf16[2,384,1536]{2,1,0:T(8,128)(2,1)S(1)} %bitcast.56, bf16[2,384,1536]{2,1,0:T(8,128)(2,1)} %bitcast.60, bf16[8,2304,384]{2,1,0:T(8,128)(2,1)} %bitcast.66, bf16[8,2304,384]{2,1,0:T(8,128)(2,1)} %bitcast.67), custom_call_target="tpu_custom_call" | custom-call | tf_op jit(solution)/shard_map/pallas_call | solution.py:152
  272.7 12.7 %shard_map.55.refs_1_ = f32[384,2304]{1,0:T(8,128)} custom-call(s32[9]{0:T(128)S(1)} %concatenate.18.scalar_ref, bf16[2,384,1536]{2,1,0:T(8,128)(2,1)S(1)} %bitcast.57, bf16[2,384,1536]{2,1,0:T(8,128)(2,1)S(1)} %bitcast.61, bf16[8,2304,384]{2,1,0:T(8,128)(2,1)} %bitcast.68, bf16[8,2304,384]{2,1,0:T(8,128)(2,1)} %bitcast.69), custom_call_target="tpu_custom_call" | custom-call | tf_op jit(solution)/shard_map/pallas_call | solution.py:152
  285.4 16.4 %all-gather.7.cloned.1.call-done = bf16[6144,384]{1,0:T(8,128)(2,1)} async-done(((bf16[768,384]{1,0:T(8,128)(2,1)}), bf16[6144,384]{1,0:T(8,128)(2,1)}) %all-gather.7.cloned.1.call-update) | async-done | bytes 4718608 | tf_op jit(solution)/shard_map/all_gather | solution.py:209
  303.5 5.9 %shard_map.60 = bf16[384,768]{1,0:T(8,128)(2,1)S(1)} custom-call(s32[9]{0:T(128)S(1)} %concatenate.20.scalar_ref, bf16[2,384,1536]{2,1,0:T(8,128)(2,1)S(1)} %bitcast.58, bf16[2,384,1536]{2,1,0:T(8,128)(2,1)S(1)} %bitcast.62, bf16[8,768,384]{2,1,0:T(8,128)(2,1)} %shard_map.58.refs_2_.refs_3_, bf16[8,768,384]{2,1,0:T(8,128)(2,1)} %shard_map.58.refs_2_.refs_3_), custom_call_target="tpu_custom_call" | custom-call | tf_op jit(solution)/shard_map/pallas_call | solution.py:152
  310.6 6.1 %shard_map.59 = f32[384,768]{1,0:T(8,128)S(1)} custom-call(s32[9]{0:T(128)S(1)} %concatenate.18.scalar_ref, bf16[2,384,1536]{2,1,0:T(8,128)(2,1)S(1)} %bitcast.59, bf16[2,384,1536]{2,1,0:T(8,128)(2,1)S(1)} %bitcast.63, bf16[8,768,384]{2,1,0:T(8,128)(2,1)} %shard_map.58.refs_2_.refs_3_, bf16[8,768,384]{2,1,0:T(8,128)(2,1)} %shard_map.58.refs_2_.refs_3_), custom_call_target="tpu_custom_call" | custom-call | tf_op jit(solution)/shard_map/pallas_call | solution.py:152
  316.7 7.4 %collective-permute-done.28 = bf16[384,768]{1,0:T(8,128)(2,1)S(1)} collective-permute-done((bf16[384,768]{1,0:T(8,128)(2,1)S(1)}, bf16[384,768]{1,0:T(8,128)(2,1)S(1)}, u32[]{:S(2)}, u32[]{:S(2)}) %collective-permute-start.28) | collective-permute-done | bytes 589856 | tf_op jit(solution)/shard_map/ppermute | solution.py:21
  324.3 1.9 add_convert_fusion
  (147 shorter events, 52.6 us)
Async XLA Ops:
  6.5 251.0 %all-gather.5.cloned.1.call-start = ((), (), s32[]{:S(2)}) async-start(), calls=%async_computation | async-start | bytes 15925248 | tf_op jit(solution)/shard_map/all_gather | solution.py:209
  15.0 36.5 %collective-permute-start.1 = (bf16[512,384]{1,0:T(8,128)(2,1)S(1)}, bf16[512,384]{1,0:T(8,128)(2,1)S(1)}, u32[]{:S(2)}, u32[]{:S(2)}) collective-permute-start(bf16[512,384]{1,0:T(8,128)(2,1)S(1)} %pad_maximum_fusion.3.refs_0_), channel_id=1, source_target_pairs={{8,0},{12,4},{0,8},{4,12},{9,1},{13,5},{1,9},{5,13},{10,2},{14,6},... | collective-permute-start | bytes 1179656 | tf_op jit(solution)/shard_map/ppermute | solution.py:21
  17.4 33.2 %collective-permute-start.2 = (bf16[512,384]{1,0:T(8,128)(2,1)S(1)}, bf16[512,384]{1,0:T(8,128)(2,1)S(1)}, u32[]{:S(2)}, u32[]{:S(2)}) collective-permute-start(bf16[512,384]{1,0:T(8,128)(2,1)S(1)} %pad_maximum_fusion.3.refs_0_), channel_id=1, source_target_pairs={{4,0},{8,4},{12,8},{0,12},{5,1},{9,5},{13,9},{1,13},{6,2},{10,6},{... | collective-permute-start | bytes 1179656 | tf_op jit(solution)/shard_map/ppermute | solution.py:21
  20.5 37.9 %collective-permute-start = (bf16[768,384]{1,0:T(8,128)(2,1)S(1)}, bf16[768,384]{1,0:T(8,128)(2,1)S(1)}, u32[]{:S(2)}, u32[]{:S(2)}) collective-permute-start(bf16[768,384]{1,0:T(8,128)(2,1)S(1)} %bitcast.64), channel_id=1, source_target_pairs={{2,0},{0,2},{3,1},{1,3},{6,4},{4,6},{7,5},{5,7},{10,8},{8,10},{11,... | collective-permute-start | bytes 1769480 | tf_op jit(solution)/shard_map/ppermute | solution.py:21
  22.5 29.7 %collective-permute-start.3 = (bf16[512,384]{1,0:T(8,128)(2,1)S(1)}, bf16[512,384]{1,0:T(8,128)(2,1)S(1)}, u32[]{:S(2)}, u32[]{:S(2)}) collective-permute-start(bf16[512,384]{1,0:T(8,128)(2,1)S(1)} %pad_maximum_fusion.3.refs_0_), channel_id=1, source_target_pairs={{12,0},{0,4},{4,8},{8,12},{13,1},{1,5},{5,9},{9,13},{14,2},{2,6},{... | collective-permute-start | bytes 1179656 | tf_op jit(solution)/shard_map/ppermute | solution.py:21
  23.8 32.6 %collective-permute-start.10 = (bf16[512,384]{1,0:T(8,128)(2,1)S(1)}, bf16[512,384]{1,0:T(8,128)(2,1)S(1)}, u32[]{:S(2)}, u32[]{:S(2)}) collective-permute-start(bf16[512,384]{1,0:T(8,128)(2,1)S(1)} %pad_maximum_fusion.3.refs_0_), channel_id=1, source_target_pairs={{16,0},{0,16},{17,1},{1,17},{18,2},{2,18},{19,3},{3,19},{20,4},{4,... | collective-permute-start | bytes 1179656 | tf_op jit(solution)/shard_map/ppermute | solution.py:21
  50.6 5.2 %collective-permute-start.14 = (bf16[256,384]{1,0:T(8,128)(2,1)S(1)}, bf16[256,384]{1,0:T(8,128)(2,1)S(1)}, u32[]{:S(2)}, u32[]{:S(2)}) collective-permute-start(bf16[256,384]{1,0:T(8,128)(2,1)S(1)} %convolution_convert_fusion.1), channel_id=1, source_target_pairs={{2,0},{0,2},{3,1},{1,3},{6,4},{4,6},{7,5},{5,7},{10,8},{8,10},{11,... | collective-permute-start | bytes 589832 | tf_op jit(solution)/shard_map/ppermute | solution.py:21
  51.6 8.4 %collective-permute-start.16 = (bf16[256,384]{1,0:T(8,128)(2,1)S(1)}, bf16[256,384]{1,0:T(8,128)(2,1)S(1)}, u32[]{:S(2)}, u32[]{:S(2)}) collective-permute-start(bf16[256,384]{1,0:T(8,128)(2,1)S(1)} %slice.12), channel_id=1, source_target_pairs={{2,0},{0,2},{3,1},{1,3},{6,4},{4,6},{7,5},{5,7},{10,8},{8,10},{11,... | collective-permute-start | bytes 589832 | tf_op jit(solution)/shard_map/ppermute | solution.py:21
  52.2 12.1 %collective-permute-start.18 = (bf16[256,384]{1,0:T(8,128)(2,1)S(1)}, bf16[256,384]{1,0:T(8,128)(2,1)}, u32[]{:S(2)}, u32[]{:S(2)}) collective-permute-start(bf16[256,384]{1,0:T(8,128)(2,1)S(1)} %slice.13), channel_id=1, source_target_pairs={{2,0},{0,2},{3,1},{1,3},{6,4},{4,6},{7,5},{5,7},{10,8},{8,10},{11,... | collective-permute-start | bytes 589832 | tf_op jit(solution)/shard_map/ppermute | solution.py:21
  55.7 12.7 %collective-permute-start.20 = (bf16[256,384]{1,0:T(8,128)(2,1)S(1)}, bf16[256,384]{1,0:T(8,128)(2,1)}, u32[]{:S(2)}, u32[]{:S(2)}) collective-permute-start(bf16[256,384]{1,0:T(8,128)(2,1)S(1)} %slice.14), channel_id=1, source_target_pairs={{2,0},{0,2},{3,1},{1,3},{6,4},{4,6},{7,5},{5,7},{10,8},{8,10},{11,... | collective-permute-start | bytes 589832 | tf_op jit(solution)/shard_map/ppermute | solution.py:21
  57.2 23.9 %collective-permute-start.11 = (bf16[512,384]{1,0:T(8,128)(2,1)S(1)}, bf16[512,384]{1,0:T(8,128)(2,1)S(1)}, u32[]{:S(2)}, u32[]{:S(2)}) collective-permute-start(bf16[512,384]{1,0:T(8,128)(2,1)S(1)} %collective-permute-done.2.refs_2_), channel_id=1, source_target_pairs={{16,0},{0,16},{17,1},{1,17},{18,2},{2,18},{19,3},{3,19},{20,4},{4,... | collective-permute-start | bytes 1179656 | tf_op jit(solution)/shard_map/ppermute | solution.py:21
  58.4 10.9 %collective-permute-start.15 = (bf16[256,384]{1,0:T(8,128)(2,1)S(1)}, bf16[256,384]{1,0:T(8,128)(2,1)S(1)}, u32[]{:S(2)}, u32[]{:S(2)}) collective-permute-start(bf16[256,384]{1,0:T(8,128)(2,1)S(1)} %collective-permute-done.14.refs_8_), channel_id=1, source_target_pairs={{16,0},{0,16},{17,1},{1,17},{18,2},{2,18},{19,3},{3,19},{20,4},{4,... | collective-permute-start | bytes 589832 | tf_op jit(solution)/shard_map/ppermute | solution.py:21
  59.9 11.5 %collective-permute-start.17 = (bf16[256,384]{1,0:T(8,128)(2,1)S(1)}, bf16[256,384]{1,0:T(8,128)(2,1)S(1)}, u32[]{:S(2)}, u32[]{:S(2)}) collective-permute-start(bf16[256,384]{1,0:T(8,128)(2,1)S(1)} %collective-permute-done.16.refs_10_), channel_id=1, source_target_pairs={{16,0},{0,16},{17,1},{1,17},{18,2},{2,18},{19,3},{3,19},{20,4},{4,... | collective-permute-start | bytes 589832 | tf_op jit(solution)/shard_map/ppermute | solution.py:21
  64.2 11.4 %collective-permute-start.19 = (bf16[256,384]{1,0:T(8,128)(2,1)}, bf16[256,384]{1,0:T(8,128)(2,1)S(1)}, u32[]{:S(2)}, u32[]{:S(2)}) collective-permute-start(bf16[256,384]{1,0:T(8,128)(2,1)} %collective-permute-done.18.refs_12_), channel_id=1, source_target_pairs={{16,0},{0,16},{17,1},{1,17},{18,2},{2,18},{19,3},{3,19},{20,4},{4,... | collective-permute-start | bytes 589832 | tf_op jit(solution)/shard_map/ppermute | solution.py:21
  68.5 11.4 %collective-permute-start.21 = (bf16[256,384]{1,0:T(8,128)(2,1)}, bf16[256,384]{1,0:T(8,128)(2,1)}, u32[]{:S(2)}, u32[]{:S(2)}) collective-permute-start(bf16[256,384]{1,0:T(8,128)(2,1)} %collective-permute-done.20.refs_14_), channel_id=1, source_target_pairs={{16,0},{0,16},{17,1},{1,17},{18,2},{2,18},{19,3},{3,19},{20,4},{4,... | collective-permute-start | bytes 589832 | tf_op jit(solution)/shard_map/ppermute | solution.py:21
  69.3 32.7 %collective-permute-start.8 = (bf16[768,384]{1,0:T(8,128)(2,1)}, bf16[768,384]{1,0:T(8,128)(2,1)}, u32[]{:S(2)}, u32[]{:S(2)}) collective-permute-start(bf16[768,384]{1,0:T(8,128)(2,1)} %shard_map.48), channel_id=1, source_target_pairs={{12,0},{0,4},{4,8},{8,12},{13,1},{1,5},{5,9},{9,13},{14,2},{2,6},{... | collective-permute-start | bytes 1769480 | tf_op jit(solution)/shard_map/ppermute | solution.py:21
  72.1 40.9 %collective-permute-start.6 = (bf16[768,384]{1,0:T(8,128)(2,1)}, bf16[768,384]{1,0:T(8,128)(2,1)}, u32[]{:S(2)}, u32[]{:S(2)}) collective-permute-start(bf16[768,384]{1,0:T(8,128)(2,1)} %shard_map.47), channel_id=1, source_target_pairs={{8,0},{12,4},{0,8},{4,12},{9,1},{13,5},{1,9},{5,13},{10,2},{14,6},... | collective-permute-start | bytes 1769480 | tf_op jit(solution)/shard_map/ppermute | solution.py:21
  76.3 40.6 %collective-permute-start.4 = (bf16[768,384]{1,0:T(8,128)(2,1)}, bf16[768,384]{1,0:T(8,128)(2,1)}, u32[]{:S(2)}, u32[]{:S(2)}) collective-permute-start(bf16[768,384]{1,0:T(8,128)(2,1)} %shard_map.46), channel_id=1, source_target_pairs={{4,0},{8,4},{12,8},{0,12},{5,1},{9,5},{13,9},{1,13},{6,2},{10,6},{... | collective-permute-start | bytes 1769480 | tf_op jit(solution)/shard_map/ppermute | solution.py:21
  79.9 9.6 %collective-permute-start.12 = (bf16[512,384]{1,0:T(8,128)(2,1)S(1)}, bf16[512,384]{1,0:T(8,128)(2,1)S(1)}, u32[]{:S(2)}, u32[]{:S(2)}) collective-permute-start(bf16[512,384]{1,0:T(8,128)(2,1)S(1)} %copy-done.12), channel_id=1, source_target_pairs={{16,0},{0,16},{17,1},{1,17},{18,2},{2,18},{19,3},{3,19},{20,4},{4,... | collective-permute-start | bytes 1179656 | tf_op jit(solution)/shard_map/ppermute | solution.py:21
  81.1 14.7 %collective-permute-start.13 = (bf16[512,384]{1,0:T(8,128)(2,1)S(1)}, bf16[512,384]{1,0:T(8,128)(2,1)S(1)}, u32[]{:S(2)}, u32[]{:S(2)}) collective-permute-start(bf16[512,384]{1,0:T(8,128)(2,1)S(1)} %copy-done.16), channel_id=1, source_target_pairs={{16,0},{0,16},{17,1},{1,17},{18,2},{2,18},{19,3},{3,19},{20,4},{4,... | collective-permute-start | bytes 1179656 | tf_op jit(solution)/shard_map/ppermute | solution.py:21
  117.0 184.8 %all-gather.7.cloned.1.call-start = ((), (), s32[]{:S(2)}) async-start(), calls=%async_computation.1 | async-start | bytes 5308416 | tf_op jit(solution)/shard_map/all_gather | solution.py:209
  120.6 7.3 %collective-permute-start.22 = (bf16[512,1536]{1,0:T(8,128)(2,1)S(1)}, bf16[512,1536]{1,0:T(8,128)(2,1)}, u32[]{:S(2)}, u32[]{:S(2)}) collective-permute-start(bf16[512,1536]{1,0:T(8,128)(2,1)S(1)} %copy-done.8), channel_id=1, source_target_pairs={{1,0},{0,1},{3,2},{2,3},{5,4},{4,5},{7,6},{6,7},{9,8},{8,9},{11,10... | collective-permute-start | bytes 4718600 | tf_op jit(solution)/shard_map/ppermute | solution.py:21
  124.7 30.7 %collective-permute-start.9 = (bf16[768,384]{1,0:T(8,128)(2,1)}, bf16[768,384]{1,0:T(8,128)(2,1)}, u32[]{:S(2)}, u32[]{:S(2)}) collective-permute-start(bf16[768,384]{1,0:T(8,128)(2,1)} %collective-permute-done.8.refs_3_), channel_id=1, source_target_pairs={{2,0},{0,2},{3,1},{1,3},{6,4},{4,6},{7,5},{5,7},{10,8},{8,10},{11,... | collective-permute-start | bytes 1769480 | tf_op jit(solution)/shard_map/ppermute | solution.py:21
  126.0 29.5 %collective-permute-start.7 = (bf16[768,384]{1,0:T(8,128)(2,1)}, bf16[768,384]{1,0:T(8,128)(2,1)}, u32[]{:S(2)}, u32[]{:S(2)}) collective-permute-start(bf16[768,384]{1,0:T(8,128)(2,1)} %collective-permute-done.6.refs_2_), channel_id=1, source_target_pairs={{2,0},{0,2},{3,1},{1,3},{6,4},{4,6},{7,5},{5,7},{10,8},{8,10},{11,... | collective-permute-start | bytes 1769480 | tf_op jit(solution)/shard_map/ppermute | solution.py:21
  126.2 39.1 %collective-permute-start.5 = (bf16[768,384]{1,0:T(8,128)(2,1)}, bf16[768,384]{1,0:T(8,128)(2,1)}, u32[]{:S(2)}, u32[]{:S(2)}) collective-permute-start(bf16[768,384]{1,0:T(8,128)(2,1)} %collective-permute-done.4.refs_1_), channel_id=1, source_target_pairs={{2,0},{0,2},{3,1},{1,3},{6,4},{4,6},{7,5},{5,7},{10,8},{8,10},{11,... | collective-permute-start | bytes 1769480 | tf_op jit(solution)/shard_map/ppermute | solution.py:21
  130.6 34.6 %copy-start.18 = (bf16[4,384,512]{2,1,0:T(8,128)(2,1)S(1)}, bf16[4,384,512]{2,1,0:T(8,128)(2,1)}, u32[]{:S(2)}) copy-start(bf16[4,384,512]{2,1,0:T(8,128)(2,1)} %get-tuple-element.8.refs_4_) | copy-start | bytes 4718596
  180.7 16.7 %collective-permute-start.23 = (bf16[2,192,1536]{2,1,0:T(8,128)(2,1)}, bf16[2,192,1536]{2,1,0:T(8,128)(2,1)}, u32[]{:S(2)}, u32[]{:S(2)}) collective-permute-start(bf16[2,192,1536]{2,1,0:T(8,128)(2,1)} %dynamic-slice_bitcast_fusion.1), channel_id=1, source_target_pairs={{1,0},{0,1},{3,2},{2,3},{5,4},{4,5},{7,6},{6,7},{9,8},{8,9},{11,10... | collective-permute-start | bytes 3538952 | tf_op jit(solution)/shard_map/ppermute | solution.py:21
  197.3 3.2 collective-permute-start.25
  199.6 27.7 %collective-permute-start.24 = (bf16[2,192,1536]{2,1,0:T(8,128)(2,1)S(1)}, bf16[2,192,1536]{2,1,0:T(8,128)(2,1)}, u32[]{:S(2)}, u32[]{:S(2)}) collective-permute-start(bf16[2,192,1536]{2,1,0:T(8,128)(2,1)S(1)} %fusion.1), channel_id=1, source_target_pairs={{16,0},{0,16},{17,1},{1,17},{18,2},{2,18},{19,3},{3,19},{20,4},{4,... | collective-permute-start | bytes 3538952 | tf_op jit(solution)/shard_map/ppermute | solution.py:21
  227.3 27.0 %collective-permute-start.26 = (bf16[2,192,1536]{2,1,0:T(8,128)(2,1)}, bf16[2,192,1536]{2,1,0:T(8,128)(2,1)}, u32[]{:S(2)}, u32[]{:S(2)}) collective-permute-start(bf16[2,192,1536]{2,1,0:T(8,128)(2,1)} %shard_map.53), channel_id=1, source_target_pairs={{16,0},{0,16},{17,1},{1,17},{18,2},{2,18},{19,3},{3,19},{20,4},{4,... | collective-permute-start | bytes 3538952 | tf_op jit(solution)/shard_map/ppermute | solution.py:21
  269.9 54.4 %collective-permute-start.27 = (bf16[384,2304]{1,0:T(8,128)(2,1)}, bf16[384,2304]{1,0:T(8,128)(2,1)}, u32[]{:S(2)}, u32[]{:S(2)}) collective-permute-start(bf16[384,2304]{1,0:T(8,128)(2,1)} %shard_map.56), channel_id=1, source_target_pairs={{2,0},{0,2},{3,1},{1,3},{6,4},{4,6},{7,5},{5,7},{10,8},{8,10},{11,... | collective-permute-start | bytes 5308424 | tf_op jit(solution)/shard_map/ppermute | solution.py:21
  309.3 14.8 %collective-permute-start.28 = (bf16[384,768]{1,0:T(8,128)(2,1)S(1)}, bf16[384,768]{1,0:T(8,128)(2,1)S(1)}, u32[]{:S(2)}, u32[]{:S(2)}) collective-permute-start(bf16[384,768]{1,0:T(8,128)(2,1)S(1)} %shard_map.60), channel_id=1, source_target_pairs={{2,0},{0,2},{3,1},{1,3},{6,4},{4,6},{7,5},{5,7},{10,8},{8,10},{11,... | collective-permute-start | bytes 1769480 | tf_op jit(solution)/shard_map/ppermute | solution.py:21
  (37 other events, 316.7 us)
Sparse Core Ops, SparseCore 0:
  117.1 131.5 all-gather.4
  250.4 51.3 all-gather.6

commit v4 on v3

--- a/solution.py
+++ b/solution.py
@@ -174,6 +174,16 @@
     proj_in = jnp.dot(tokens, basis_in, preferred_element_type=f32).astype(bf16)
     proj_out = jnp.dot(out_grads, basis_out, preferred_element_type=f32).astype(bf16)
     both = jnp.concatenate([proj_in, proj_out], axis=0)
+    blocks = pair * pair
+    share = quarter // (blocks * ny)
+    in_view = basis_in.reshape(nz, blocks, ny, share, cols)
+    def in_block(s):
+        to = (at["z"] + nz - s) % nz
+        block = lax.dynamic_slice(in_view, (to, 0, at["y"], 0, 0), (1, blocks, 1, share, cols))
+        return block.reshape(eighth, cols)
+
+    early = fetch(in_block(1), "z", 1)
+    both = after(both, early)
     order = [0] + sorted(range(1, nz), key=lambda s: -min(s, nz - s))
     groups, others, links = {}, {}, []
     for s in order:
@@ -185,15 +195,10 @@
     left, left_other, right = pack([groups[s] for s in every], [others[s] for s in every], rows)
     rights = [right, fetch(right, "c")]
 
-    blocks = pair * pair
-    share = quarter // (blocks * ny)
-    in_view = basis_in.reshape(nz, blocks, ny, share, cols)
     in_own, in_other = {}, {}
     for s in order:
-        to = (at["z"] + nz - s) % nz
-        block = lax.dynamic_slice(in_view, (to, 0, at["y"], 0, 0), (1, blocks, 1, share, cols))
-        block = block.reshape(eighth, cols)
-        in_own[s] = fetch(after(block, *links, in_other[0]), "z", s) if s else block
+        block = in_block(s) if s != 1 else early
+        in_own[s] = fetch(after(block, *links, in_other[0]), "z", s) if s > 1 else block
         in_other[s] = fetch(in_own[s], "x")
     in_own = [in_own[s] for s in range(nz)]
     in_other = [in_other[s] for s in range(nz)]
@@ -201,7 +206,7 @@
     out_rows = width // ny
     cuts = [out_rows * sum(shares[:k]) // sum(shares) // 128 * 128 for k in range(len(shares))] + [out_rows]
     sizes = [b - a for a, b in zip(cuts, cuts[1:])]
-    wides, gate = [], [*in_own[1:], left]
+    wides, gate = [], [*in_own[1:], *[w for s in order[:-1] for w in others[s][1:]], others[order[-1]][0], *[w for s in order for w in groups[s][1:]]]
     for k in range(len(shares)):
         first = at["y"] * out_rows + cuts[k]
         raw = lax.dynamic_slice_in_dim(basis_out, first, sizes[k], 0)
@@ -214,7 +219,8 @@
     for h in range(2):
         part = mix(in_other, left_other, rights, at["c"], h, 1, bf16, own)
         view = part.reshape(pair, pair, share, -1)
-        away = fetch(take(view, 1, 1 - at["c"]), "c")
+        away = take(view, 1, 1 - at["c"])
+        away = jnp.stack([fetch(away[i], "c") for i in range(pair)])
         mine = (take(view, 1, at["c"]).astype(f32) + away.astype(f32)).astype(bf16)
         got = gather(after(mine, *got[1:]) if h else mine, "y")
         full = jnp.stack(

time: 339 us -> 328 us (0.968)
  waiting for transfers between devices: 155 us -> 137 us
  starting transfers between devices: 26.7 us -> 31.7 us
    ppermute x29 -> x31, waiting for transfers between devices: 139 us -> 120 us  [fetch(): return lax.ppermute(value, axis, pairs(lax.axis_size(axis), shift))]
    ppermute x29 -> x31, starting transfers between devices: 26.5 us -> 31.4 us  [fetch(): return lax.ppermute(value, axis, pairs(lax.axis_size(axis), shift))]
    unnamed x76 -> x92, local copies, waits for them, and re-layouts: 17.1 us -> 16.4 us
  transfers between devices with their start and end apart: 31 -> 33, of which waited for: 18 -> 22; matrix products, arithmetic and copies ran while one was open for 6% -> 8% of each run, Pallas kernels for 27% -> 29%
where the time goes in v4:
time: 328 us; the launch traced here: 322 us
  waiting for transfers between devices  137 us (42%)
  Pallas kernels  92.5 us (28%)
  local copies, waits for them, and re-layouts  31.8 us (10%)
  starting transfers between devices  31.7 us (10%)
  between operations  13.7 us (4%)
  other arithmetic  11.9 us (4%)
  matrix products  3.64 us (1%)
    ppermute x31, waiting for transfers between devices, fetch(): return lax.ppermute(value, axis, pairs(lax.axis_size(axis), shift))  120 us
    pallas_call x3, Pallas kernels, mix(): pl.pallas_call(body, out_shape=jax.ShapeDtypeStruct((n, 2 * runs * tj), k...  50.6 us
    pallas_call x4, Pallas kernels, expand(): pl.pallas_call(body, out_shape=jax.ShapeDtypeStruct((n, wide), kind), gri...  37.1 us
    ppermute x31, starting transfers between devices, fetch(): return lax.ppermute(value, axis, pairs(lax.axis_size(axis), shift))  31.4 us
    all_gather x2, waiting for transfers between devices, shards(): wides.append(lax.all_gather(raw, ('z', 'c'), axis=0))  16.5 us
    unnamed x92, local copies, waits for them, and re-layouts  16.4 us
  transfers between devices with their start and end apart: 33, of which 22 were waited for; matrix products, arithmetic and copies ran while one was open for 8% of the time, Pallas kernels for 29%

profile of v4, /device:TPU:9, one launch (start us, length us, event | category | flops | bytes accessed | tf_op | source)
XLA Modules:
  0.0 321.8 jit_solution(6853848763805158784)
XLA Ops:
  6.5 3.0 constant_dynamic-slice_fusion.2
  16.7 8.1 %collective-permute-done.1.refs_1_ = bf16[768,384]{1,0:T(8,128)(2,1)} collective-permute-done((bf16[768,384]{1,0:T(8,128)(2,1)S(1)}, bf16[768,384]{1,0:T(8,128)(2,1)}, u32[]{:S(2)}, u32[]{:S(2)}) %collective-permute-start.1) | collective-permute-done | bytes 589856 | tf_op jit(solution)/shard_map/ppermute | solution.py:21
  26.0 2.9 collective-permute-start.3
  28.9 2.4 collective-permute-start.5
  33.8 4.6 %collective-permute-done.14.refs_8_ = bf16[256,384]{1,0:T(8,128)(2,1)S(1)} collective-permute-done((bf16[256,384]{1,0:T(8,128)(2,1)S(1)}, bf16[256,384]{1,0:T(8,128)(2,1)S(1)}, u32[]{:S(2)}, u32[]{:S(2)}) %collective-permute-start.14) | collective-permute-done | bytes 196640 | tf_op jit(solution)/shard_map/ppermute | solution.py:21
  40.5 13.5 %collective-permute-done.3.refs_1_.refs_4_ = bf16[512,384]{1,0:T(8,128)(2,1)S(1)} collective-permute-done((bf16[512,384]{1,0:T(8,128)(2,1)}, bf16[512,384]{1,0:T(8,128)(2,1)S(1)}, u32[]{:S(2)}, u32[]{:S(2)}) %collective-permute-start.3) | collective-permute-done | bytes 393248 | tf_op jit(solution)/shard_map/ppermute | solution.py:21
  55.3 7.1 %collective-permute-done.5.refs_3_.refs_6_ = bf16[512,384]{1,0:T(8,128)(2,1)S(1)} collective-permute-done((bf16[512,384]{1,0:T(8,128)(2,1)}, bf16[512,384]{1,0:T(8,128)(2,1)S(1)}, u32[]{:S(2)}, u32[]{:S(2)}) %collective-permute-start.5) | collective-permute-done | bytes 393248 | tf_op jit(solution)/shard_map/ppermute | solution.py:21
  65.3 2.2 collective-permute-done.16.refs_10_
  67.5 4.2 %collective-permute-done.18.refs_12_ = bf16[256,384]{1,0:T(8,128)(2,1)} collective-permute-done((bf16[256,384]{1,0:T(8,128)(2,1)S(1)}, bf16[256,384]{1,0:T(8,128)(2,1)}, u32[]{:S(2)}, u32[]{:S(2)}) %collective-permute-start.18) | collective-permute-done | bytes 196640 | tf_op jit(solution)/shard_map/ppermute | solution.py:21
  73.8 2.1 collective-permute-done.20.refs_14_.refs_7_
  78.6 2.9 constant_dynamic-slice_fusion.1.refs_0_
  81.5 2.5 collective-permute-done.13.refs_7_.refs_11_
  84.0 4.2 %collective-permute-done.17.refs_11_.refs_6_ = bf16[256,384]{1,0:T(8,128)(2,1)S(1)} collective-permute-done((bf16[256,384]{1,0:T(8,128)(2,1)}, bf16[256,384]{1,0:T(8,128)(2,1)S(1)}, u32[]{:S(2)}, u32[]{:S(2)}) %collective-permute-start.17) | collective-permute-done | bytes 196640 | tf_op jit(solution)/shard_map/ppermute | solution.py:21
  88.2 4.2 %collective-permute-done.19.refs_13_.refs_5_ = bf16[256,384]{1,0:T(8,128)(2,1)S(1)} collective-permute-done((bf16[256,384]{1,0:T(8,128)(2,1)}, bf16[256,384]{1,0:T(8,128)(2,1)S(1)}, u32[]{:S(2)}, u32[]{:S(2)}) %collective-permute-start.19) | collective-permute-done | bytes 196640 | tf_op jit(solution)/shard_map/ppermute | solution.py:21
  92.4 10.7 %collective-permute-done.8.refs_3_ = bf16[768,384]{1,0:T(8,128)(2,1)S(1)} collective-permute-done((bf16[768,384]{1,0:T(8,128)(2,1)}, bf16[768,384]{1,0:T(8,128)(2,1)S(1)}, u32[]{:S(2)}, u32[]{:S(2)}) %collective-permute-start.8) | collective-permute-done | bytes 589856 | tf_op jit(solution)/shard_map/ppermute | solution.py:21
  107.5 3.5 %collective-permute-done.21.refs_15_ = bf16[256,384]{1,0:T(8,128)(2,1)S(1)} collective-permute-done((bf16[256,384]{1,0:T(8,128)(2,1)}, bf16[256,384]{1,0:T(8,128)(2,1)S(1)}, u32[]{:S(2)}, u32[]{:S(2)}) %collective-permute-start.21) | collective-permute-done | bytes 196640 | tf_op jit(solution)/shard_map/ppermute | solution.py:21
  116.8 4.7 %shard_map.49 = (bf16[4,384,512]{2,1,0:T(8,128)(2,1)}, bf16[4,384,512]{2,1,0:T(8,128)(2,1)}, bf16[512,1536]{1,0:T(8,128)(2,1)}) custom-call(bf16[512,384]{1,0:T(8,128)(2,1)S(1)} %copy-done.12, bf16[512,384]{1,0:T(8,128)(2,1)S(1)} %copy-done.21, bf16[512,384]{1,0:T(8,128)(2,1)S(1)} %copy-done.14, bf16[512,384]{1,0:T(8,128)(2,1)S(1)} %copy-done.23, ...), custom_call_target="tpu_custom_call" | custom-call | tf_op jit(solution)/shard_map/pallas_call | solution.py:61
  121.5 4.5 %collective-permute-start.22 = (bf16[512,1536]{1,0:T(8,128)(2,1)}, bf16[512,1536]{1,0:T(8,128)(2,1)S(1)}, u32[]{:S(2)}, u32[]{:S(2)}) collective-permute-start(bf16[512,1536]{1,0:T(8,128)(2,1)} %get-tuple-element.9.refs_5_), channel_id=1, source_target_pairs={{1,0},{0,1},{3,2},{2,3},{5,4},{4,5},{7,6},{6,7},{9,8},{8,9},{11,10... | collective-permute-start | bytes 4718600 | tf_op jit(solution)/shard_map/ppermute | solution.py:21
  133.3 24.3 %shard_map.50.refs_7_ = f32[768,3072]{1,0:T(8,128)} custom-call(s32[1]{0:T(128)} %bitcast.9.first_ref, bf16[768,384]{1,0:T(8,128)(2,1)} %bitcast.11.refs_0_, bf16[768,384]{1,0:T(8,128)(2,1)} %collective-permute-done.1.refs_1_, bf16[768,384]{1,0:T(8,128)(2,1)S(1)} %copy-done.9, bf16[768,384]{1,0:T(8,128)(2,1)S(1)} %copy-done.11, ...), custom_call_target="tpu_custom_call" | custom-call | tf_op jit(solution)/shard_map/pallas_call | solution.py:99
  157.5 9.0 %collective-permute-done.9.refs_3_ = bf16[768,384]{1,0:T(8,128)(2,1)} collective-permute-done((bf16[768,384]{1,0:T(8,128)(2,1)S(1)}, bf16[768,384]{1,0:T(8,128)(2,1)}, u32[]{:S(2)}, u32[]{:S(2)}) %collective-permute-start.9) | collective-permute-done | bytes 589856 | tf_op jit(solution)/shard_map/ppermute | solution.py:21
  166.6 13.2 %shard_map.51 = bf16[768,1536]{1,0:T(8,128)(2,1)} custom-call(s32[1]{0:T(128)} %bitcast.9.first_ref, bf16[768,384]{1,0:T(8,128)(2,1)} %collective-permute-done.refs_4_.refs_0_, bf16[768,384]{1,0:T(8,128)(2,1)} %collective-permute-done.2.refs_1_, bf16[768,384]{1,0:T(8,128)(2,1)} %collective-permute-done.7.refs_2_, ...), custom_call_target="tpu_custom_call" | custom-call | tf_op jit(solution)/shard_map/pallas_call | solution.py:99
  179.8 2.4 dynamic-slice_bitcast_fusion.3
  189.4 13.2 %shard_map.52 = bf16[768,1536]{1,0:T(8,128)(2,1)} custom-call(s32[1]{0:T(128)} %bitcast.9.first_ref, bf16[768,384]{1,0:T(8,128)(2,1)} %collective-permute-done.refs_4_.refs_0_, bf16[768,384]{1,0:T(8,128)(2,1)} %collective-permute-done.2.refs_1_, bf16[768,384]{1,0:T(8,128)(2,1)} %collective-permute-done.7.refs_2_, ...), custom_call_target="tpu_custom_call" | custom-call | tf_op jit(solution)/shard_map/pallas_call | solution.py:99
  208.9 6.6 %collective-permute-done.25.refs_1_ = bf16[2,192,1536]{2,1,0:T(8,128)(2,1)} collective-permute-done((bf16[2,192,1536]{2,1,0:T(8,128)(2,1)S(1)}, bf16[2,192,1536]{2,1,0:T(8,128)(2,1)}, u32[]{:S(2)}, u32[]{:S(2)}) %collective-permute-start.25) | collective-permute-done | bytes 1179680 | tf_op jit(solution)/shard_map/ppermute | solution.py:21
  216.9 2.1 select_bitcast_fusion.3
  219.4 22.7 %collective-permute-done.28 = bf16[2,192,1536]{2,1,0:T(8,128)(2,1)} collective-permute-done((bf16[2,192,1536]{2,1,0:T(8,128)(2,1)}, bf16[2,192,1536]{2,1,0:T(8,128)(2,1)}, u32[]{:S(2)}, u32[]{:S(2)}) %collective-permute-start.28) | collective-permute-done | bytes 1179680 | tf_op jit(solution)/shard_map/ppermute | solution.py:21
  245.3 12.5 %shard_map.56 = bf16[384,2304]{1,0:T(8,128)(2,1)} custom-call(s32[9]{0:T(128)S(1)} %concatenate.20.scalar_ref, bf16[2,384,1536]{2,1,0:T(8,128)(2,1)S(1)} %bitcast.62, bf16[2,384,1536]{2,1,0:T(8,128)(2,1)} %bitcast.66, bf16[8,2304,384]{2,1,0:T(8,128)(2,1)} %bitcast.70, bf16[8,2304,384]{2,1,0:T(8,128)(2,1)} %bitcast.71), custom_call_target="tpu_custom_call" | custom-call | tf_op jit(solution)/shard_map/pallas_call | solution.py:152
  259.6 12.6 %shard_map.55.refs_1_ = f32[384,2304]{1,0:T(8,128)} custom-call(s32[9]{0:T(128)S(1)} %concatenate.18.scalar_ref, bf16[2,384,1536]{2,1,0:T(8,128)(2,1)S(1)} %bitcast.63, bf16[2,384,1536]{2,1,0:T(8,128)(2,1)S(1)} %bitcast.67, bf16[8,2304,384]{2,1,0:T(8,128)(2,1)} %bitcast.72, bf16[8,2304,384]{2,1,0:T(8,128)(2,1)} %bitcast.73), custom_call_target="tpu_custom_call" | custom-call | tf_op jit(solution)/shard_map/pallas_call | solution.py:152
  272.2 16.5 %all-gather.7.cloned.1.call-done = bf16[6144,384]{1,0:T(8,128)(2,1)} async-done(((bf16[768,384]{1,0:T(8,128)(2,1)}), bf16[6144,384]{1,0:T(8,128)(2,1)}) %all-gather.7.cloned.1.call-update) | async-done | bytes 4718608 | tf_op jit(solution)/shard_map/all_gather | solution.py:214
  290.5 5.9 %shard_map.60 = bf16[384,768]{1,0:T(8,128)(2,1)S(1)} custom-call(s32[9]{0:T(128)S(1)} %concatenate.20.scalar_ref, bf16[2,384,1536]{2,1,0:T(8,128)(2,1)S(1)} %bitcast.64, bf16[2,384,1536]{2,1,0:T(8,128)(2,1)S(1)} %bitcast.68, bf16[8,768,384]{2,1,0:T(8,128)(2,1)} %shard_map.58.refs_2_.refs_3_, bf16[8,768,384]{2,1,0:T(8,128)(2,1)} %shard_map.58.refs_2_.refs_3_), custom_call_target="tpu_custom_call" | custom-call | tf_op jit(solution)/shard_map/pallas_call | solution.py:152
  297.6 6.2 %shard_map.59 = f32[384,768]{1,0:T(8,128)S(1)} custom-call(s32[9]{0:T(128)S(1)} %concatenate.18.scalar_ref, bf16[2,384,1536]{2,1,0:T(8,128)(2,1)S(1)} %bitcast.65, bf16[2,384,1536]{2,1,0:T(8,128)(2,1)S(1)} %bitcast.69, bf16[8,768,384]{2,1,0:T(8,128)(2,1)} %shard_map.58.refs_2_.refs_3_, bf16[8,768,384]{2,1,0:T(8,128)(2,1)} %shard_map.58.refs_2_.refs_3_), custom_call_target="tpu_custom_call" | custom-call | tf_op jit(solution)/shard_map/pallas_call | solution.py:152
  303.8 7.3 %collective-permute-done.30 = bf16[384,768]{1,0:T(8,128)(2,1)S(1)} collective-permute-done((bf16[384,768]{1,0:T(8,128)(2,1)S(1)}, bf16[384,768]{1,0:T(8,128)(2,1)S(1)}, u32[]{:S(2)}, u32[]{:S(2)}) %collective-permute-start.30) | collective-permute-done | bytes 589856 | tf_op jit(solution)/shard_map/ppermute | solution.py:21
  (169 shorter events, 66.3 us)
Async XLA Ops:
  6.5 238.8 %all-gather.5.cloned.1.call-start = ((), (), s32[]{:S(2)}) async-start(), calls=%async_computation | async-start | bytes 15925248 | tf_op jit(solution)/shard_map/all_gather | solution.py:214
  9.6 23.9 %collective-permute-start = (bf16[768,384]{1,0:T(8,128)(2,1)}, bf16[768,384]{1,0:T(8,128)(2,1)}, u32[]{:S(2)}, u32[]{:S(2)}) collective-permute-start(bf16[768,384]{1,0:T(8,128)(2,1)} %bitcast.11.refs_0_), channel_id=1, source_target_pairs={{2,0},{0,2},{3,1},{1,3},{6,4},{4,6},{7,5},{5,7},{10,8},{8,10},{11,... | collective-permute-start | bytes 1769480 | tf_op jit(solution)/shard_map/ppermute | solution.py:21
  10.8 14.0 %collective-permute-start.1 = (bf16[768,384]{1,0:T(8,128)(2,1)S(1)}, bf16[768,384]{1,0:T(8,128)(2,1)}, u32[]{:S(2)}, u32[]{:S(2)}) collective-permute-start(bf16[768,384]{1,0:T(8,128)(2,1)S(1)} %bitcast.84), channel_id=1, source_target_pairs={{4,0},{8,4},{12,8},{0,12},{5,1},{9,5},{13,9},{1,13},{6,2},{10,6},{... | collective-permute-start | bytes 1769480 | tf_op jit(solution)/shard_map/ppermute | solution.py:21
  24.8 14.5 %collective-permute-start.4 = (bf16[512,384]{1,0:T(8,128)(2,1)}, bf16[512,384]{1,0:T(8,128)(2,1)S(1)}, u32[]{:S(2)}, u32[]{:S(2)}) collective-permute-start(bf16[512,384]{1,0:T(8,128)(2,1)} %shard_map.46.refs_0_), channel_id=1, source_target_pairs={{4,0},{8,4},{12,8},{0,12},{5,1},{9,5},{13,9},{1,13},{6,2},{10,6},{... | collective-permute-start | bytes 1179656 | tf_op jit(solution)/shard_map/ppermute | solution.py:21
  26.0 28.0 %collective-permute-start.3 = (bf16[512,384]{1,0:T(8,128)(2,1)}, bf16[512,384]{1,0:T(8,128)(2,1)S(1)}, u32[]{:S(2)}, u32[]{:S(2)}) collective-permute-start(bf16[512,384]{1,0:T(8,128)(2,1)} %shard_map.46.refs_0_), channel_id=1, source_target_pairs={{8,0},{12,4},{0,8},{4,12},{9,1},{13,5},{1,9},{5,13},{10,2},{14,6},... | collective-permute-start | bytes 1179656 | tf_op jit(solution)/shard_map/ppermute | solution.py:21
  28.9 33.5 %collective-permute-start.5 = (bf16[512,384]{1,0:T(8,128)(2,1)}, bf16[512,384]{1,0:T(8,128)(2,1)S(1)}, u32[]{:S(2)}, u32[]{:S(2)}) collective-permute-start(bf16[512,384]{1,0:T(8,128)(2,1)} %shard_map.46.refs_0_), channel_id=1, source_target_pairs={{12,0},{0,4},{4,8},{8,12},{13,1},{1,5},{5,9},{9,13},{14,2},{2,6},{... | collective-permute-start | bytes 1179656 | tf_op jit(solution)/shard_map/ppermute | solution.py:21
  31.3 31.4 %collective-permute-start.10 = (bf16[512,384]{1,0:T(8,128)(2,1)}, bf16[512,384]{1,0:T(8,128)(2,1)S(1)}, u32[]{:S(2)}, u32[]{:S(2)}) collective-permute-start(bf16[512,384]{1,0:T(8,128)(2,1)} %shard_map.46.refs_0_), channel_id=1, source_target_pairs={{16,0},{0,16},{17,1},{1,17},{18,2},{2,18},{19,3},{3,19},{20,4},{4,... | collective-permute-start | bytes 1179656 | tf_op jit(solution)/shard_map/ppermute | solution.py:21
  33.5 4.9 %collective-permute-start.14 = (bf16[256,384]{1,0:T(8,128)(2,1)S(1)}, bf16[256,384]{1,0:T(8,128)(2,1)S(1)}, u32[]{:S(2)}, u32[]{:S(2)}) collective-permute-start(bf16[256,384]{1,0:T(8,128)(2,1)S(1)} %slice.36), channel_id=1, source_target_pairs={{2,0},{0,2},{3,1},{1,3},{6,4},{4,6},{7,5},{5,7},{10,8},{8,10},{11,... | collective-permute-start | bytes 589832 | tf_op jit(solution)/shard_map/ppermute | solution.py:21
  38.4 26.2 %collective-permute-start.15 = (bf16[256,384]{1,0:T(8,128)(2,1)S(1)}, bf16[256,384]{1,0:T(8,128)(2,1)S(1)}, u32[]{:S(2)}, u32[]{:S(2)}) collective-permute-start(bf16[256,384]{1,0:T(8,128)(2,1)S(1)} %collective-permute-done.14.refs_8_), channel_id=1, source_target_pairs={{16,0},{0,16},{17,1},{1,17},{18,2},{2,18},{19,3},{3,19},{20,4},{4,... | collective-permute-start | bytes 589832 | tf_op jit(solution)/shard_map/ppermute | solution.py:21
  39.3 37.8 %collective-permute-start.11 = (bf16[512,384]{1,0:T(8,128)(2,1)S(1)}, bf16[512,384]{1,0:T(8,128)(2,1)S(1)}, u32[]{:S(2)}, u32[]{:S(2)}) collective-permute-start(bf16[512,384]{1,0:T(8,128)(2,1)S(1)} %collective-permute-done.4.refs_2_), channel_id=1, source_target_pairs={{16,0},{0,16},{17,1},{1,17},{18,2},{2,18},{19,3},{3,19},{20,4},{4,... | collective-permute-start | bytes 1179656 | tf_op jit(solution)/shard_map/ppermute | solution.py:21
  54.0 23.4 %collective-permute-start.12 = (bf16[512,384]{1,0:T(8,128)(2,1)S(1)}, bf16[512,384]{1,0:T(8,128)(2,1)S(1)}, u32[]{:S(2)}, u32[]{:S(2)}) collective-permute-start(bf16[512,384]{1,0:T(8,128)(2,1)S(1)} %collective-permute-done.3.refs_1_.refs_4_), channel_id=1, source_target_pairs={{16,0},{0,16},{17,1},{1,17},{18,2},{2,18},{19,3},{3,19},{20,4},{4,... | collective-permute-start | bytes 1179656 | tf_op jit(solution)/shard_map/ppermute | solution.py:21
  62.4 5.0 %collective-permute-start.16 = (bf16[256,384]{1,0:T(8,128)(2,1)S(1)}, bf16[256,384]{1,0:T(8,128)(2,1)}, u32[]{:S(2)}, u32[]{:S(2)}) collective-permute-start(bf16[256,384]{1,0:T(8,128)(2,1)S(1)} %slice.37), channel_id=1, source_target_pairs={{2,0},{0,2},{3,1},{1,3},{6,4},{4,6},{7,5},{5,7},{10,8},{8,10},{11,... | collective-permute-start | bytes 589832 | tf_op jit(solution)/shard_map/ppermute | solution.py:21
  62.7 9.0 %collective-permute-start.18 = (bf16[256,384]{1,0:T(8,128)(2,1)S(1)}, bf16[256,384]{1,0:T(8,128)(2,1)}, u32[]{:S(2)}, u32[]{:S(2)}) collective-permute-start(bf16[256,384]{1,0:T(8,128)(2,1)S(1)} %slice.38), channel_id=1, source_target_pairs={{2,0},{0,2},{3,1},{1,3},{6,4},{4,6},{7,5},{5,7},{10,8},{8,10},{11,... | collective-permute-start | bytes 589832 | tf_op jit(solution)/shard_map/ppermute | solution.py:21
  64.6 11.3 %collective-permute-start.20 = (bf16[256,384]{1,0:T(8,128)(2,1)}, bf16[256,384]{1,0:T(8,128)(2,1)}, u32[]{:S(2)}, u32[]{:S(2)}) collective-permute-start(bf16[256,384]{1,0:T(8,128)(2,1)} %slice.39), channel_id=1, source_target_pairs={{2,0},{0,2},{3,1},{1,3},{6,4},{4,6},{7,5},{5,7},{10,8},{8,10},{11,... | collective-permute-start | bytes 589832 | tf_op jit(solution)/shard_map/ppermute | solution.py:21
  67.5 24.9 %collective-permute-start.6 = (bf16[768,384]{1,0:T(8,128)(2,1)}, bf16[768,384]{1,0:T(8,128)(2,1)S(1)}, u32[]{:S(2)}, u32[]{:S(2)}) collective-permute-start(bf16[768,384]{1,0:T(8,128)(2,1)} %shard_map.47), channel_id=1, source_target_pairs={{8,0},{12,4},{0,8},{4,12},{9,1},{13,5},{1,9},{5,13},{10,2},{14,6},... | collective-permute-start | bytes 1769480 | tf_op jit(solution)/shard_map/ppermute | solution.py:21
  71.7 31.4 %collective-permute-start.8 = (bf16[768,384]{1,0:T(8,128)(2,1)}, bf16[768,384]{1,0:T(8,128)(2,1)S(1)}, u32[]{:S(2)}, u32[]{:S(2)}) collective-permute-start(bf16[768,384]{1,0:T(8,128)(2,1)} %shard_map.48), channel_id=1, source_target_pairs={{12,0},{0,4},{4,8},{8,12},{13,1},{1,5},{5,9},{9,13},{14,2},{2,6},{... | collective-permute-start | bytes 1769480 | tf_op jit(solution)/shard_map/ppermute | solution.py:21
  75.9 8.1 %collective-permute-start.13 = (bf16[512,384]{1,0:T(8,128)(2,1)S(1)}, bf16[512,384]{1,0:T(8,128)(2,1)S(1)}, u32[]{:S(2)}, u32[]{:S(2)}) collective-permute-start(bf16[512,384]{1,0:T(8,128)(2,1)S(1)} %copy-done.18), channel_id=1, source_target_pairs={{16,0},{0,16},{17,1},{1,17},{18,2},{2,18},{19,3},{3,19},{20,4},{4,... | collective-permute-start | bytes 1179656 | tf_op jit(solution)/shard_map/ppermute | solution.py:21
  77.1 11.0 %collective-permute-start.17 = (bf16[256,384]{1,0:T(8,128)(2,1)}, bf16[256,384]{1,0:T(8,128)(2,1)S(1)}, u32[]{:S(2)}, u32[]{:S(2)}) collective-permute-start(bf16[256,384]{1,0:T(8,128)(2,1)} %collective-permute-done.16.refs_10_), channel_id=1, source_target_pairs={{16,0},{0,16},{17,1},{1,17},{18,2},{2,18},{19,3},{3,19},{20,4},{4,... | collective-permute-start | bytes 589832 | tf_op jit(solution)/shard_map/ppermute | solution.py:21
  77.4 15.0 %collective-permute-start.19 = (bf16[256,384]{1,0:T(8,128)(2,1)}, bf16[256,384]{1,0:T(8,128)(2,1)S(1)}, u32[]{:S(2)}, u32[]{:S(2)}) collective-permute-start(bf16[256,384]{1,0:T(8,128)(2,1)} %collective-permute-done.18.refs_12_), channel_id=1, source_target_pairs={{16,0},{0,16},{17,1},{1,17},{18,2},{2,18},{19,3},{3,19},{20,4},{4,... | collective-permute-start | bytes 589832 | tf_op jit(solution)/shard_map/ppermute | solution.py:21
  104.0 184.8 %all-gather.7.cloned.1.call-start = ((), (), s32[]{:S(2)}) async-start(), calls=%async_computation.1 | async-start | bytes 5308416 | tf_op jit(solution)/shard_map/all_gather | solution.py:214
  106.2 4.8 %collective-permute-start.21 = (bf16[256,384]{1,0:T(8,128)(2,1)}, bf16[256,384]{1,0:T(8,128)(2,1)S(1)}, u32[]{:S(2)}, u32[]{:S(2)}) collective-permute-start(bf16[256,384]{1,0:T(8,128)(2,1)} %collective-permute-done.20.refs_14_.refs_7_), channel_id=1, source_target_pairs={{16,0},{0,16},{17,1},{1,17},{18,2},{2,18},{19,3},{3,19},{20,4},{4,... | collective-permute-start | bytes 589832 | tf_op jit(solution)/shard_map/ppermute | solution.py:21
  121.5 7.7 %collective-permute-start.22 = (bf16[512,1536]{1,0:T(8,128)(2,1)}, bf16[512,1536]{1,0:T(8,128)(2,1)S(1)}, u32[]{:S(2)}, u32[]{:S(2)}) collective-permute-start(bf16[512,1536]{1,0:T(8,128)(2,1)} %get-tuple-element.9.refs_5_), channel_id=1, source_target_pairs={{1,0},{0,1},{3,2},{2,3},{5,4},{4,5},{7,6},{6,7},{9,8},{8,9},{11,10... | collective-permute-start | bytes 4718600 | tf_op jit(solution)/shard_map/ppermute | solution.py:21
  126.0 31.5 %collective-permute-start.2 = (bf16[768,384]{1,0:T(8,128)(2,1)}, bf16[768,384]{1,0:T(8,128)(2,1)}, u32[]{:S(2)}, u32[]{:S(2)}) collective-permute-start(bf16[768,384]{1,0:T(8,128)(2,1)} %collective-permute-done.1.refs_1_), channel_id=1, source_target_pairs={{2,0},{0,2},{3,1},{1,3},{6,4},{4,6},{7,5},{5,7},{10,8},{8,10},{11,... | collective-permute-start | bytes 1769480 | tf_op jit(solution)/shard_map/ppermute | solution.py:21
  126.3 31.3 %collective-permute-start.7 = (bf16[768,384]{1,0:T(8,128)(2,1)S(1)}, bf16[768,384]{1,0:T(8,128)(2,1)}, u32[]{:S(2)}, u32[]{:S(2)}) collective-permute-start(bf16[768,384]{1,0:T(8,128)(2,1)S(1)} %copy-done.9), channel_id=1, source_target_pairs={{2,0},{0,2},{3,1},{1,3},{6,4},{4,6},{7,5},{5,7},{10,8},{8,10},{11,... | collective-permute-start | bytes 1769480 | tf_op jit(solution)/shard_map/ppermute | solution.py:21
  127.5 39.1 %collective-permute-start.9 = (bf16[768,384]{1,0:T(8,128)(2,1)S(1)}, bf16[768,384]{1,0:T(8,128)(2,1)}, u32[]{:S(2)}, u32[]{:S(2)}) collective-permute-start(bf16[768,384]{1,0:T(8,128)(2,1)S(1)} %copy-done.11), channel_id=1, source_target_pairs={{2,0},{0,2},{3,1},{1,3},{6,4},{4,6},{7,5},{5,7},{10,8},{8,10},{11,... | collective-permute-start | bytes 1769480 | tf_op jit(solution)/shard_map/ppermute | solution.py:21
  182.2 2.8 collective-permute-start.24
  183.0 3.1 collective-permute-start.23
  188.1 27.4 %collective-permute-start.25 = (bf16[2,192,1536]{2,1,0:T(8,128)(2,1)S(1)}, bf16[2,192,1536]{2,1,0:T(8,128)(2,1)}, u32[]{:S(2)}, u32[]{:S(2)}) collective-permute-start(bf16[2,192,1536]{2,1,0:T(8,128)(2,1)S(1)} %fusion.1), channel_id=1, source_target_pairs={{16,0},{0,16},{17,1},{1,17},{18,2},{2,18},{19,3},{3,19},{20,4},{4,... | collective-permute-start | bytes 3538952 | tf_op jit(solution)/shard_map/ppermute | solution.py:21
  204.7 2.8 collective-permute-start.26
  215.5 26.6 %collective-permute-start.28 = (bf16[2,192,1536]{2,1,0:T(8,128)(2,1)}, bf16[2,192,1536]{2,1,0:T(8,128)(2,1)}, u32[]{:S(2)}, u32[]{:S(2)}) collective-permute-start(bf16[2,192,1536]{2,1,0:T(8,128)(2,1)} %shard_map.53), channel_id=1, source_target_pairs={{16,0},{0,16},{17,1},{1,17},{18,2},{2,18},{19,3},{3,19},{20,4},{4,... | collective-permute-start | bytes 3538952 | tf_op jit(solution)/shard_map/ppermute | solution.py:21
  257.8 53.4 %collective-permute-start.29 = (bf16[384,2304]{1,0:T(8,128)(2,1)}, bf16[384,2304]{1,0:T(8,128)(2,1)}, u32[]{:S(2)}, u32[]{:S(2)}) collective-permute-start(bf16[384,2304]{1,0:T(8,128)(2,1)} %shard_map.56), channel_id=1, source_target_pairs={{2,0},{0,2},{3,1},{1,3},{6,4},{4,6},{7,5},{5,7},{10,8},{8,10},{11,... | collective-permute-start | bytes 5308424 | tf_op jit(solution)/shard_map/ppermute | solution.py:21
  296.3 14.8 %collective-permute-start.30 = (bf16[384,768]{1,0:T(8,128)(2,1)S(1)}, bf16[384,768]{1,0:T(8,128)(2,1)S(1)}, u32[]{:S(2)}, u32[]{:S(2)}) collective-permute-start(bf16[384,768]{1,0:T(8,128)(2,1)S(1)} %shard_map.60), channel_id=1, source_target_pairs={{2,0},{0,2},{3,1},{1,3},{6,4},{4,6},{7,5},{5,7},{10,8},{8,10},{11,... | collective-permute-start | bytes 1769480 | tf_op jit(solution)/shard_map/ppermute | solution.py:21
  (47 other events, 365.3 us)
Sparse Core Ops, SparseCore 0:
  104.1 131.5 all-gather.4
  237.4 51.3 all-gather.6
